TPU v7x, 512 devices: a whole 4x8x8 slice. The times are simulated.
512 devices in a mesh: dp: 64 (over x, y, core), proto: 8 (over z).
Axes of the slice: x: 4, y: 8, z: 8, core: 2. Of those that a mesh axis runs over, the one named last changes fastest.
Arguments:
- teacher_feats: bfloat16 [8192, 256], P('dp'), may hold values from -3 to 3
- student_feats: bfloat16 [8192, 256], P('dp'), may hold values from -0.375 to 0.375
- prototypes: bfloat16 [256, 32768], P(None, 'proto'), may hold values from -3 to 3
Outputs:
- grad_features: float32 [8192, 256], P('dp')
- grad_prototypes: float32 [256, 32768], P('dp', 'proto')
All inputs are finite; a program needn't handle non-finite values.
Results may differ from a plain program's by a relative error of at most 0.0039.
Values sent between devices are 32-bit elements; how exact they have to be, the bound alone decides.
A program may use at most 64 MiB of HBM per device.

v0:
```python
import jax
import jax.numpy as jnp
from jax import lax
from jax.sharding import PartitionSpec as P

PROTOS = 32768
ITERS = 3


EPS = 1e-06
TEMP_T = 0.07
TEMP_S = 0.1


def unit_rows(features):
    widened = features.astype(jnp.float32)
    inverse = lax.rsqrt(jnp.sum(widened * widened, 1, keepdims=True) + EPS)
    return ((widened * inverse).astype(jnp.bfloat16), inverse)


def shards(teacher_feats, student_feats, prototypes):
    full_w = prototypes.astype(jnp.float32)
    unit_proto = (full_w * lax.rsqrt(jnp.sum(full_w * full_w, 0, keepdims=True) + EPS)).astype(
        jnp.bfloat16
    )
    teacher_unit, _ = unit_rows(teacher_feats)
    student_unit, student_inv = unit_rows(student_feats)
    student_exp = jnp.exp(
        jnp.dot(student_unit, unit_proto, preferred_element_type=jnp.float32) / TEMP_S
    )
    student_total = lax.psum(jnp.sum(student_exp, 1), "proto")
    teacher_exp = jnp.exp(
        jnp.dot(teacher_unit, unit_proto, preferred_element_type=jnp.float32) / TEMP_T
    )
    row_scale = jnp.ones((teacher_exp.shape[0],), jnp.float32)
    col_scale = jnp.ones((teacher_exp.shape[1],), jnp.float32)
    for iteration in range(ITERS):
        local_cols = jnp.dot(row_scale, teacher_exp, precision=lax.Precision.HIGHEST)
        col_scale = 1.0 / lax.psum(local_cols, "dp")
        local_rows = jnp.dot(teacher_exp, col_scale, precision=lax.Precision.HIGHEST)
        row_scale = 1.0 / lax.psum(local_rows, "proto")
    targets = teacher_exp * col_scale[None, :] * row_scale[:, None]
    probs = student_exp / student_total[:, None]
    grad_logit = (PROTOS / 64.0 * (probs - targets) / TEMP_S).astype(jnp.bfloat16)
    grad_prototypes = lax.psum_scatter(
        lax.dot_general(
            student_unit, grad_logit, (((0,), (0,)), ((), ())), preferred_element_type=jnp.float32
        ),
        "dp",
        scatter_dimension=0,
        tiled=True,
    )
    local_unit = lax.dot_general(
        grad_logit, unit_proto, (((1,), (1,)), ((), ())), preferred_element_type=jnp.float32
    )
    grad_unit = lax.psum(local_unit, "proto")
    unit_wide = student_unit.astype(jnp.float32)
    projected = jnp.sum(unit_wide * grad_unit, 1, keepdims=True)
    grad_features = (grad_unit - unit_wide * projected) * student_inv
    return (grad_features, grad_prototypes)


def solution(mesh):
    placed = (P("dp", None), P("dp", None), P(None, "proto"))
    return jax.shard_map(
        shards,
        mesh=mesh,
        in_specs=placed,
        out_specs=(P("dp", None), P("dp", "proto")),
        check_vma=False,
    )
```

profile of v0, /device:TPU:1, one launch (start us, length us, event | category | flops | bytes accessed | tf_op | source)
XLA Modules:
  0.0 1106.7 jit_solution(33871931846091385)
XLA Ops:
  7.2 2.2 fusion.2
  9.7 0.7 fusion
  10.4 2.1 fusion.33
  12.5 1.1 fusion.23
  13.6 247.4 %psum.57 = f32[4096]{0:T(1024)S(1)} all-reduce(f32[4096]{0:T(1024)S(1)} %bitcast.35), channel_id=1, replica_groups=mesh['dp'=64,'proto'=8] {'dp'}, use_global_device_ids=true, to_apply=%region_5.0 | all-reduce | flops 4096 | bytes 32768 | tf_op jit(solution)/shard_map/psum | solution.py:39
  261.0 1.7 convolution_bitcast_fusion.2
  262.7 19.1 %psum.58 = f32[128]{0:T(128)S(1)} all-reduce(f32[128]{0:T(128)S(1)} %convolution_bitcast_fusion.2), channel_id=1, replica_groups=mesh['dp'=64,'proto'=8] {'proto'}, use_global_device_ids=true, to_apply=%region_6.0 | all-reduce | flops 128 | bytes 1024 | tf_op jit(solution)/shard_map/psum | solution.py:41
  281.8 1.1 fusion.19
  282.9 249.9 %psum.59 = f32[4096]{0:T(1024)S(1)} all-reduce(f32[4096]{0:T(1024)S(1)} %bitcast.32), channel_id=1, replica_groups=mesh['dp'=64,'proto'=8] {'dp'}, use_global_device_ids=true, to_apply=%region_7.0 | all-reduce | flops 4096 | bytes 32768 | tf_op jit(solution)/shard_map/psum | solution.py:39
  532.8 1.7 convolution_bitcast_fusion.1
  534.6 10.7 psum.60
  545.2 1.1 fusion.17
  546.3 249.6 %psum.61 = f32[4096]{0:T(1024)S(1)} all-reduce(f32[4096]{0:T(1024)S(1)} %bitcast.34), channel_id=1, replica_groups=mesh['dp'=64,'proto'=8] {'dp'}, use_global_device_ids=true, to_apply=%region_9.0 | all-reduce | flops 4096 | bytes 32768 | tf_op jit(solution)/shard_map/psum | solution.py:39
  796.0 1.7 convolution_bitcast_fusion
  797.7 12.4 %all-reduce.1 = (f32[128]{0:T(128)S(1)}, f32[128]{0:T(128)S(1)}) all-reduce(f32[128]{0:T(128)S(1)} %convolution_bitcast_fusion, f32[128]{0:T(128)S(1)} %get-tuple-element.4), channel_id=1, replica_groups=mesh['dp'=64,'proto'=8] {'proto'}, use_global_device_ids=true, to_apply=%region_10.0 | all-reduce | flops 256 | bytes 2048 | tf_op jit(solution)/shard_map/psum | solution.py:41
  810.1 2.3 multiply_convert_fusion
  812.4 1.5 fusion.4
  814.0 2.8 fusion.30
  816.8 1.3 dynamic-slice
  818.7 67.8 %all-reduce.5.cloned.1.call-done = f32[128,256]{1,0:T(8,128)} async-done(((f32[128,256]{1,0:T(8,128)}), f32[128,256]{1,0:T(8,128)}) %all-reduce.5.cloned.1.call-update) | async-done | bytes 131088 | tf_op jit(solution)/shard_map/psum | solution.py:56
  886.6 1.1 fusion.12
  887.6 1.7 fusion.14
  889.3 209.0 %all-reduce.7.cloned.1.call-done = f32[256,4096]{1,0:T(8,128)} async-done(((f32[256,4096]{1,0:T(8,128)}), f32[256,4096]{1,0:T(8,128)}) %all-reduce.7.cloned.1.call-update) | async-done | bytes 4194320
  1098.3 1.5 constant_dynamic-slice_fusion
  (21 shorter events, 0.4 us)
Async XLA Ops:
  7.2 2.3 copy-start.3
  7.2 2.4 copy-start.2
  7.2 879.4 %all-reduce.5.cloned.1.call-start = ((), (), s32[]{:S(2)}) async-start(), calls=%async_computation | async-start | bytes 262144 | tf_op jit(solution)/shard_map/psum | solution.py:56
  7.2 2.5 copy-start
  810.1 2.4 copy-start.1
  814.0 284.3 %all-reduce.7.cloned.1.call-start = ((), (), s32[]{:S(2)}) async-start(), calls=%async_computation.1 | async-start | bytes 8388608
Sparse Core Ops, SparseCore 0:
  814.1 72.4 all-reduce.4
  890.5 207.7 all-reduce.6
where the time goes:
time: 1110 us
  blocking collectives  789 us (71%)
  waiting for transfers between devices  277 us (25%)
  matrix products  15.5 us (1%)
  between operations  14.8 us (1%)
    psum x3, blocking collectives, shards(): col_scale = 1.0 / lax.psum(local_cols, 'dp')  747 us
    unnamed x3, waiting for transfers between devices  209 us
    psum x1, waiting for transfers between devices, shards(): grad_unit = lax.psum(local_unit, 'proto')  67.8 us
    psum x3, blocking collectives, shards(): row_scale = 1.0 / lax.psum(local_rows, 'proto')  42.2 us
  transfers between devices with their start and end apart: 2, of which 2 were waited for; matrix products, arithmetic and copies ran while one was open for 1% of the time, Pallas kernels for 0%

commit v1 on v0

v1 whole, which is shorter than its diff:
```python
import functools

import jax
import jax.numpy as jnp
from jax import lax
from jax.experimental import pallas as pl
from jax.experimental.pallas import tpu as pltpu
from jax.sharding import PartitionSpec as P

EPS = 1e-06
INV_T = 1.0 / 0.07
INV_S = 1.0 / 0.1
ITERS = 3
NX, NY, NC, NZ = 4, 8, 2, 8
B = 128
D = 256
K = 4096
CH = K // 256
TL = K // 128
KB = K // (NX * NC)
SCALE = 32768 / 64.0 / 0.1
MESH = pl.DeviceIdType.MESH

UP, XX, YY, DN, ZZ = (0, 3, 6, 9, 12)
G1, G2, TT, RR, GP, ZR, ZA = range(15, 22)
GROUPS = 22


def dot(a, b):
    return jnp.dot(a, b, preferred_element_type=jnp.float32)


def unit_rows(raw):
    wide = raw.astype(jnp.float32)
    inv = lax.rsqrt(jnp.sum(wide * wide, 1, keepdims=True) + EPS)
    return (wide * inv).astype(jnp.bfloat16), inv


def body(
    t_ref, s_ref, w_ref, gf_out, gp_out,
    WU, E, SE, F, ETB, ESB, SBT, GB, GPS, GPR, GFS, GFR, GFO, GFA,
    CS, CR, XS, XR, YS, YR, CF, ZS, ZRV, TS, RB, ITB, RW, ITW, ssem, rsem,
):
    dp = lax.axis_index("dp")
    z = lax.axis_index("proto")
    c = lax.rem(dp, 2)
    y = lax.rem(dp // 2, NY)
    x = dp // (2 * NY)

    def dev(dx, dy, dc, dz):
        return (
            (lax.rem(x + dx, NX) * NY + lax.rem(y + dy, NY)) * NC + lax.rem(c + dc, NC),
            lax.rem(z + dz, NZ),
        )

    mate = dev(0, 0, 1, 0)

    def send(src, dst, group, to):
        pltpu.make_async_remote_copy(
            src, dst, ssem.at[group], rsem.at[group], device_id=to, device_id_type=MESH
        ).start()

    def arrived(ref, group):
        pltpu.make_async_remote_copy(
            ref, ref, ssem.at[group], rsem.at[group], device_id=mate, device_id_type=MESH
        ).wait_recv()

    def sent(ref, group):
        pltpu.make_async_remote_copy(
            ref, ref, ssem.at[group], rsem.at[group], device_id=mate, device_id_type=MESH
        ).wait_send()

    barrier = pltpu.get_barrier_semaphore()

    def greet(i, carry):
        to = dev(i // (NY * NC), lax.rem(i // NC, NY), lax.rem(i, NC), 0)
        pl.semaphore_signal(barrier, inc=1, device_id=to, device_id_type=MESH)
        return carry

    lax.fori_loop(1, NX * NY * NC, greet, 0)
    for k in range(1, NZ):
        pl.semaphore_signal(barrier, inc=1, device_id=dev(0, 0, 0, k), device_id_type=MESH)

    t_unit, _ = unit_rows(t_ref[...])
    s_unit, _ = unit_rows(s_ref[...])
    F[0, :B, :] = t_unit.astype(jnp.float32)
    F[0, B:, :] = s_unit.astype(jnp.float32)

    def first(j, carry):
        w = w_ref[:, pl.ds(pl.multiple_of(j * 256, 256), 256)].astype(jnp.float32)
        w = (w * lax.rsqrt(jnp.sum(w * w, 0, keepdims=True) + EPS)).astype(jnp.bfloat16)
        WU[j] = w
        e = jnp.exp(dot(t_unit, w) * INV_T)
        E[2 * j] = e[:, :128]
        E[2 * j + 1] = e[:, 128:]
        CS[0, pl.ds(2 * j, 1), :] = jnp.sum(e[:, :128], 0, keepdims=True)
        CS[0, pl.ds(2 * j + 1, 1), :] = jnp.sum(e[:, 128:], 0, keepdims=True)
        return carry

    lax.fori_loop(0, CH, first, 0, unroll=2)
    pl.semaphore_wait(barrier, NX * NY * NC - 1 + NZ - 1)

    def student():
        def step(j, acc):
            e = jnp.exp(dot(s_unit, WU[j]) * INV_S)
            SE[2 * j] = e[:, :128]
            SE[2 * j + 1] = e[:, 128:]
            return acc + e[:, :128] + e[:, 128:]

        acc = lax.fori_loop(0, CH, step, jnp.zeros((B, 128), jnp.float32), unroll=2)
        return jnp.sum(acc.T, 0, keepdims=True)

    def gather_x():
        for k in range(1, NX):
            send(F.at[0], F.at[k], G1, dev(k, 0, 0, 0))

    def line_block(j, carry):
        tb = F[j, :B, :].astype(jnp.bfloat16)
        sw = F[j, B:, :]
        sb = sw.astype(jnp.bfloat16)
        SBT[j] = sw.T.astype(jnp.bfloat16)
        own = (x * NC + c) * (KB // 256)
        for h in range(KB // 256):
            w = WU[own + h]
            ETB[j, h] = jnp.exp(dot(tb, w) * INV_T)
            ESB[j, h] = jnp.exp(dot(sb, w) * INV_S)
        return carry

    def columns(i):
        @pl.when(c == 0)
        def _():
            send(CS.at[i], CR.at[i], UP + i, mate)

        if i == 0:
            total = student()
            ZS[0, 1:2, :] = total

        @pl.when(c == 1)
        def _():
            arrived(CR.at[i], UP + i)
            XS[i] = CS[i] + CR[i]
            for k in range(1, NX):
                send(XS.at[i], XR.at[i, k - 1], XX + i, dev(k, 0, 0, 0))
            arrived(XR.at[i], XX + i)
            YS[i] = (XS[i] + XR[i, 0]) + (XR[i, 1] + XR[i, 2])
            for k in range(1, NY):
                send(YS.at[i], YR.at[i, k - 1], YY + i, dev(0, k, 0, 0))
            if i == 0:
                gather_x()

        if i == 1:
            arrived(F.at[pl.ds(1, NX - 1)], G1)
            send(F.at[pl.ds(0, NX)], F.at[pl.ds(NX, NX)], G2, mate)
            lax.fori_loop(0, NX, line_block, 0)
        if i == 2:
            arrived(F.at[pl.ds(NX, NX)], G2)
            lax.fori_loop(NX, 2 * NX, line_block, 0)
            arrived(TS.at[pl.ds(1, 7)], TT)
            for j in range(2 * NX):
                ITB[j] = jnp.broadcast_to(TS[j] * SCALE, (128, B)).T

        @pl.when(c == 1)
        def _():
            arrived(YR.at[i], YY + i)
            total = YS[i]
            for k in range(NY - 1):
                total = total + YR[i, k]
            CF[i] = 1.0 / total
            send(CF.at[i], CF.at[i], DN + i, mate)

        @pl.when(c == 0)
        def _():
            arrived(CF.at[i], DN + i)
            if i == 0:
                gather_x()

    def rows(i):
        def step(t, acc):
            return acc + E[t] * CF[i, pl.ds(t, 1), :]

        acc = lax.fori_loop(0, TL, step, jnp.zeros((B, 128), jnp.float32), unroll=4)
        ZS[i, 0:1, :] = jnp.sum(acc.T, 0, keepdims=True)
        for k in range(1, NZ):
            send(ZS.at[i], ZRV.at[i, k - 1], ZZ + i, dev(0, 0, 0, k))
        arrived(ZRV.at[i], ZZ + i)
        total = ZS[i]
        for k in range(NZ - 1):
            total = total + ZRV[i, k]
        return 1.0 / total

    def spread(ref, group):
        for k in range(1, 2 * NX):
            send(ref.at[0], ref.at[k], group, dev(k % NX, 0, k // NX, 0))

    for i in range(ITERS):
        columns(i)
        if i == 0:
            ZS[1] = jnp.zeros((2, 128), jnp.float32)
            ZS[2] = jnp.zeros((2, 128), jnp.float32)
        inv = rows(i)
        if i == 0:
            TS[0] = inv[1:2, :]
            spread(TS, TT)
            ITW[...] = jnp.broadcast_to(inv[1:2, :] * SCALE, (128, B)).T
        if i < ITERS - 1:
            RW[...] = jnp.broadcast_to(inv[0:1, :], (128, B)).T

            def scaled(t, carry):
                CS[i + 1, pl.ds(t, 1), :] = jnp.sum(E[t] * RW[...], 0, keepdims=True)
                return carry

            lax.fori_loop(0, TL, scaled, 0, unroll=4)
        else:
            RB[0] = inv[0:1, :]
            spread(RB, RR)
            RW[...] = jnp.broadcast_to(inv[0:1, :] * SCALE, (128, B)).T

    last = ITERS - 1

    def feature(j, acc):
        g = [
            (SE[2 * j + h] * ITW[...] - (E[2 * j + h] * CF[last, pl.ds(2 * j + h, 1), :]) * RW[...]).astype(jnp.bfloat16)
            for h in range(2)
        ]
        return acc + lax.dot_general(
            jnp.concatenate(g, 1), WU[j], (((1,), (1,)), ((), ())), preferred_element_type=jnp.float32
        )

    GFA[...] = lax.fori_loop(0, CH, feature, jnp.zeros((B, D), jnp.float32), unroll=2)
    for k in range(NZ):
        GFS[k] = GFA[16 * k:16 * k + 16, :]
    for k in range(1, NZ):
        send(GFS.at[lax.rem(z + k, NZ)], GFR.at[k - 1], ZR, dev(0, 0, 0, k))

    arrived(RB.at[pl.ds(1, 7)], RR)
    first_tile = (x * NC + c) * (KB // 128)

    def line_grad(j, carry):
        rb = jnp.broadcast_to(RB[j] * SCALE, (128, B)).T
        for q in range(KB // 128):
            h, part = q // 2, pl.ds(128 * (q % 2), 128)
            col = CF[last, pl.ds(first_tile + q, 1), :]
            g = ESB[j, h, :, part] * ITB[j] - (ETB[j, h, :, part] * col) * rb
            GB[j, :, 128 * q:128 * q + 128] = g.astype(jnp.bfloat16)
        return carry

    lax.fori_loop(0, 2 * NX, line_grad, 0)
    for h in range(KB // 256):
        acc = jnp.zeros((D, 256), jnp.float32)
        for p in range(NX):
            lhs = jnp.concatenate([SBT[2 * p], SBT[2 * p + 1]], 1)
            rhs = jnp.concatenate(
                [GB[2 * p, :, 256 * h:256 * h + 256], GB[2 * p + 1, :, 256 * h:256 * h + 256]], 0
            )
            acc = acc + dot(lhs, rhs)
        GPS[:, :, 256 * h:256 * h + 256] = acc.reshape(D // 4, 4, 256)

    def scatter(i, carry):
        to = dev(i // (NY * NC), lax.rem(i // NC, NY), lax.rem(i, NC), 0)
        send(GPS.at[to[0]], GPR.at[i], GP, to)
        return carry

    lax.fori_loop(1, NX * NY * NC, scatter, 0)

    arrived(GFR, ZR)
    mine = pl.ds(pl.multiple_of(z * 16, 16), 16)
    u, inv = unit_rows(s_ref[mine, :])
    u = u.astype(jnp.float32)
    total = GFS[z]
    for k in range(NZ - 1):
        total = total + GFR[k]
    GFO[0] = (total - u * jnp.sum(u * total, 1, keepdims=True)) * inv
    for k in range(1, NZ):
        send(GFO.at[0], GFO.at[k], ZA, dev(0, 0, 0, k))
    gf_out[mine, :] = GFO[0]

    arrived(GPR.at[pl.ds(1, NX * NY * NC - 1)], GP)
    GPR[0] = GPS[dp]
    for dx in range(NX):
        for dc in range(NC):
            total = GPR[dx * NY * NC + dc]
            for dy in range(1, NY):
                total = total + GPR[(dx * NY + dy) * NC + dc]
            at = (lax.rem(x + NX - dx, NX) * NC + lax.rem(c + dc, NC)) * KB
            gp_out[:, pl.ds(pl.multiple_of(at, KB), KB)] = total

    arrived(GFO.at[pl.ds(1, NZ - 1)], ZA)
    for k in range(1, NZ):
        at = lax.rem(z + NZ - k, NZ) * 16
        gf_out[pl.ds(pl.multiple_of(at, 16), 16), :] = GFO[k]

    for i in range(ITERS):
        @pl.when(c == 0)
        def _():
            sent(CS.at[i], UP + i)

        @pl.when(c == 1)
        def _():
            sent(XR.at[i], XX + i)
            sent(YR.at[i], YY + i)
            sent(CF.at[i], DN + i)

        sent(ZRV.at[i], ZZ + i)
    sent(F.at[pl.ds(1, NX - 1)], G1)
    sent(F.at[pl.ds(0, NX)], G2)
    sent(TS.at[pl.ds(1, 7)], TT)
    sent(RB.at[pl.ds(1, 7)], RR)
    sent(GPR.at[pl.ds(1, NX * NY * NC - 1)], GP)
    sent(GFR, ZR)
    sent(GFO.at[pl.ds(1, NZ - 1)], ZA)


def shards(teacher, student, protos):
    f32, bf16 = jnp.float32, jnp.bfloat16
    vm = pltpu.VMEM
    scratch = [
        vm((CH, D, 256), bf16),
        vm((TL, B, 128), f32),
        vm((TL, B, 128), f32),
        vm((2 * NX, 2 * B, D), f32),
        vm((2 * NX, KB // 256, B, 256), f32),
        vm((2 * NX, KB // 256, B, 256), f32),
        vm((2 * NX, D, B), bf16),
        vm((2 * NX, B, KB), bf16),
        vm((64, 4, KB), f32),
        vm((64, 4, KB), f32),
        vm((NZ, 16, D), f32),
        vm((NZ - 1, 16, D), f32),
        vm((NZ, 16, D), f32),
        vm((B, D), f32),
        vm((ITERS, TL, 128), f32),
        vm((ITERS, TL, 128), f32),
        vm((ITERS, TL, 128), f32),
        vm((ITERS, NX - 1, TL, 128), f32),
        vm((ITERS, TL, 128), f32),
        vm((ITERS, NY - 1, TL, 128), f32),
        vm((ITERS, TL, 128), f32),
        vm((ITERS, 2, 128), f32),
        vm((ITERS, NZ - 1, 2, 128), f32),
        vm((2 * NX, 1, 128), f32),
        vm((2 * NX, 1, 128), f32),
        vm((2 * NX, B, 128), f32),
        vm((B, 128), f32),
        vm((B, 128), f32),
        pltpu.SemaphoreType.DMA((GROUPS,)),
        pltpu.SemaphoreType.DMA((GROUPS,)),
    ]
    whole = pl.BlockSpec(memory_space=pltpu.VMEM)
    return pl.pallas_call(
        body,
        out_shape=(jax.ShapeDtypeStruct((B, D), f32), jax.ShapeDtypeStruct((4, K), f32)),
        in_specs=[whole] * 3,
        out_specs=(whole, whole),
        scratch_shapes=scratch,
        compiler_params=pltpu.CompilerParams(
            collective_id=0, has_side_effects=True, vmem_limit_bytes=48 * 2**20
        ),
    )(teacher, student, protos)


def solution(mesh):
    placed = (P("dp", None), P("dp", None), P(None, "proto"))
    return jax.shard_map(
        shards,
        mesh=mesh,
        in_specs=placed,
        out_specs=(P("dp", None), P("dp", "proto")),
        check_vma=False,
    )
```

time: 1110 us -> 87.6 us (0.08)
  blocking collectives: 789 us -> 0 us
  waiting for transfers between devices: 277 us -> 0 us
  Pallas kernels: 0 us -> 82.2 us
  matrix products: 15.5 us -> 0 us
  between operations: 14.8 us -> 0.65 us
    psum x6 -> x0, blocking collectives: 789 us -> none  [the longest x3 747 us: shards(): col_scale = 1.0 / lax.psum(local_cols, 'dp')]
    unnamed x3 -> x0, waiting for transfers between devices: 209 us -> none
    pallas_call x0 -> x1, Pallas kernels: none -> 82.2 us  [shards(): pl.pallas_call(body, out_shape=(jax.ShapeDtypeStruct((B, D), f32), jax.Sh...]
    psum x1 -> x0, waiting for transfers between devices: 67.8 us -> none  [shards(): grad_unit = lax.psum(local_unit, 'proto')]
    dot_general x10 -> x0, matrix products: 15.5 us -> none  [the longest x3 5.17 us: shards(): jnp.dot(teacher_exp, col_scale, precision=lax.Precision.HIGHEST)]
  transfers between devices with their start and end apart: 2 -> 0, of which waited for: 2 -> 0; matrix products, arithmetic and copies ran while one was open for 1% -> 0% of each run, Pallas kernels for 0% -> 0%
where the time goes in v1:
time: 87.6 us; the launch traced here: 87.4 us
  Pallas kernels  82.2 us (94%)
  local copies, waits for them, and re-layouts  4.55 us (5%)
    pallas_call x1, Pallas kernels, shards(): pl.pallas_call(body, out_shape=(jax.ShapeDtypeStruct((B, D), f32), jax.Sh...  82.2 us
    unnamed x8, local copies, waits for them, and re-layouts  4.55 us

profile of v1, /device:TPU:1, one launch (start us, length us, event | category | flops | bytes accessed | tf_op | source)
XLA Modules:
  0.0 87.4 jit_solution(15404109348688212778)
XLA Ops:
  0.6 0.0 copy-start
  0.6 1.6 %copy-done = bf16[256,4096]{1,0:T(8,128)(2,1)S(1)} copy-done((bf16[256,4096]{1,0:T(8,128)(2,1)S(1)}, bf16[256,4096]{1,0:T(8,128)(2,1)}, u32[]{:S(2)}) %copy-start) | copy-done | bytes 2097176
  2.2 0.0 copy-start.1
  2.2 0.8 copy-done.1
  3.1 0.0 copy-start.2
  3.1 0.8 copy-done.2
  3.9 82.2 %shard_map.50 = (f32[128,256]{1,0:T(8,128)S(1)}, f32[4,4096]{1,0:T(4,128)S(1)}) custom-call(bf16[128,256]{1,0:T(8,128)(2,1)S(1)} %copy-done.1, bf16[128,256]{1,0:T(8,128)(2,1)S(1)} %copy-done.2, bf16[256,4096]{1,0:T(8,128)(2,1)S(1)} %copy-done), custom_call_target="tpu_custom_call" | custom-call | tf_op jit(solution)/shard_map/pallas_call | solution.py:349
  86.1 0.7 copy.7
  86.7 0.6 copy.8
Async XLA Ops:
  0.6 1.6 %copy-start = (bf16[256,4096]{1,0:T(8,128)(2,1)S(1)}, bf16[256,4096]{1,0:T(8,128)(2,1)}, u32[]{:S(2)}) copy-start(bf16[256,4096]{1,0:T(8,128)(2,1)} %w_ref.1) | copy-start | bytes 6291460
  2.2 0.8 copy-start.1
  3.1 0.8 copy-start.2

commit v2 on v1

v2 whole, which is shorter than its diff:
```python
import functools

import jax
import jax.numpy as jnp
from jax import lax
from jax.experimental import pallas as pl
from jax.experimental.pallas import tpu as pltpu
from jax.sharding import PartitionSpec as P

EPS = 1e-06
INV_T = 1.0 / 0.07
INV_S = 1.0 / 0.1
ITERS = 3
NX, NY, NC, NZ = 4, 8, 2, 8
B = 128
D = 256
K = 4096
CH = K // 256
TL = K // 128
KB = K // (NX * NC)
SCALE = 32768 / 64.0 / 0.1
MESH = pl.DeviceIdType.MESH

UP, DN, G0, G1, G2, TZ, T1, T2, RM, GP, ZR, ZA = range(12)
XX, YY, ZZ = (12, 15, 18)
GROUPS = 21
LOADS = 4


def dot(a, b):
    return jnp.dot(a, b, preferred_element_type=jnp.float32)


def unit_rows(raw):
    wide = raw.astype(jnp.float32)
    inv = lax.rsqrt(jnp.sum(wide * wide, 1, keepdims=True) + EPS)
    return (wide * inv).astype(jnp.bfloat16), inv


def across(row):
    return jnp.broadcast_to(row, (128, 128)).T


def body(
    t_hbm, s_hbm, w_hbm, gf_out, gp_out,
    t_ref, s_ref, w_ref, WU, E, SE, F, ETB, ESB, SBT, GB, GPS, GPR, GFS, GFR, GFO, GFA,
    CS, CR, XS, XR, YS, YR, CF, ZS, ZRV, ZL, TZS, TZR, TS, RB, RBM, ITB, RW, ITW, lsem, ssem, rsem,
):
    dp = lax.axis_index("dp")
    z = lax.axis_index("proto")
    c = lax.rem(dp, 2)
    y = lax.rem(dp // 2, NY)
    x = dp // (2 * NY)

    def dev(dx, dy, dc, dz):
        return (
            (lax.rem(x + dx, NX) * NY + lax.rem(y + dy, NY)) * NC + lax.rem(c + dc, NC),
            lax.rem(z + dz, NZ),
        )

    mate = dev(0, 0, 1, 0)

    def send(src, dst, group, to):
        pltpu.make_async_remote_copy(
            src, dst, ssem.at[group], rsem.at[group], device_id=to, device_id_type=MESH
        ).start()

    def arrived(ref, group):
        pltpu.make_async_remote_copy(
            ref, ref, ssem.at[group], rsem.at[group], device_id=mate, device_id_type=MESH
        ).wait_recv()

    def sent(ref, group):
        pltpu.make_async_remote_copy(
            ref, ref, ssem.at[group], rsem.at[group], device_id=mate, device_id_type=MESH
        ).wait_send()

    loads = [
        pltpu.make_async_copy(t_hbm, t_ref, lsem.at[0]),
        pltpu.make_async_copy(s_hbm, s_ref, lsem.at[1]),
    ]
    for piece in range(LOADS):
        cols = pl.ds(piece * (K // LOADS), K // LOADS)
        loads.append(pltpu.make_async_copy(w_hbm.at[:, cols], w_ref.at[:, cols], lsem.at[2 + piece]))
    for load in loads:
        load.start()

    peers = [dev(0, 0, 1, 0)]
    peers += [dev(k, 0, 0, 0) for k in range(1, NX)]
    peers += [dev(0, k, 0, 0) for k in range(1, NY)]
    peers += [dev(0, 0, 0, k) for k in range(1, NZ)]
    barrier = pltpu.get_barrier_semaphore()
    for to in peers:
        pl.semaphore_signal(barrier, inc=1, device_id=to, device_id_type=MESH)

    loads[0].wait()
    t_unit, _ = unit_rows(t_ref[...])
    F[0, :B, :] = t_unit.astype(jnp.float32)

    def first(j, carry):
        w = w_ref[:, pl.ds(pl.multiple_of(j * 256, 256), 256)].astype(jnp.float32)
        w = (w * lax.rsqrt(jnp.sum(w * w, 0, keepdims=True) + EPS)).astype(jnp.bfloat16)
        WU[j] = w
        e = jnp.exp(dot(t_unit, w) * INV_T)
        E[2 * j, :B] = e[:, :128]
        E[2 * j + 1, :B] = e[:, 128:]
        CS[pl.ds(2 * j, 1), :] = jnp.sum(e[:, :128], 0, keepdims=True)
        CS[pl.ds(2 * j + 1, 1), :] = jnp.sum(e[:, 128:], 0, keepdims=True)
        return carry

    per = CH // LOADS
    for piece in range(LOADS):
        loads[2 + piece].wait()
        lax.fori_loop(piece * per, piece * per + per, first, 0, unroll=True)
    loads[1].wait()
    s_unit, _ = unit_rows(s_ref[...])
    F[0, B:, :] = s_unit.astype(jnp.float32)
    pl.semaphore_wait(barrier, len(peers))

    def student():
        def step(j, acc):
            e = jnp.exp(dot(F[0, B:, :].astype(jnp.bfloat16), WU[j]) * INV_S)
            SE[2 * j] = e[:, :128]
            SE[2 * j + 1] = e[:, 128:]
            return acc + e[:, :128] + e[:, 128:]

        acc = lax.fori_loop(0, CH, step, jnp.zeros((B, 128), jnp.float32), unroll=4)
        TZS[...] = jnp.sum(acc.T, 0, keepdims=True)
        for k in range(1, NZ):
            send(TZS, TZR.at[k - 1], TZ, dev(0, 0, 0, k))

    def student_totals():
        arrived(TZR, TZ)
        total = TZS[...]
        for k in range(NZ - 1):
            total = total + TZR[k]
        TS[0] = SCALE / total
        ITW[...] = across(TS[0])
        for k in range(1, NX):
            send(TS.at[0], TS.at[k], T1, dev(k, 0, 0, 0))

    def hand_totals():
        arrived(TS.at[pl.ds(1, NX - 1)], T1)
        send(TS.at[pl.ds(0, NX)], TS.at[pl.ds(NX, NX)], T2, mate)

    def line_totals():
        arrived(TS.at[pl.ds(NX, NX)], T2)
        for j in range(2 * NX):
            ITB[j] = across(TS[j])

    def gather_x():
        for k in range(1, NX):
            send(F.at[0], F.at[k], G1, dev(k, 0, 0, 0))

    def hand_blocks():
        arrived(F.at[pl.ds(1, NX - 1)], G1)
        send(F.at[pl.ds(1, NX - 1)], F.at[pl.ds(NX + 1, NX - 1)], G2, mate)

    own = (x * NC + c) * (KB // 256)

    def line_block(j, carry):
        tb = F[j, :B, :].astype(jnp.bfloat16)
        sw = F[j, B:, :]
        sb = sw.astype(jnp.bfloat16)
        SBT[j] = sw.T.astype(jnp.bfloat16)
        for h in range(KB // 256):
            w = WU[own + h]
            ETB[j, h] = jnp.exp(dot(tb, w) * INV_T)
            ESB[j, h] = jnp.exp(dot(sb, w) * INV_S)
        return carry

    def blocks(lo, hi):
        lax.fori_loop(lo, hi, line_block, 0)

    last = ITERS - 1

    @pl.when(c == 0)
    def _():
        send(CS, CR, UP, mate)
        send(F.at[0], F.at[NX], G0, mate)
        student()
        blocks(0, 1)
        student_totals()
        gather_x()
        arrived(F.at[NX], G0)
        blocks(NX, NX + 1)
        hand_totals()
        hand_blocks()
        blocks(1, NX)
        arrived(F.at[pl.ds(NX + 1, NX - 1)], G2)
        blocks(NX + 1, 2 * NX)
        line_totals()
        arrived(CF.at[last], DN)
        arrived(RB, RM)

    @pl.when(c == 1)
    def _():
        def mate_exp(j, carry):
            e = jnp.exp(dot(F[NX, :B, :].astype(jnp.bfloat16), WU[j]) * INV_T)
            E[2 * j, B:] = e[:, :128]
            E[2 * j + 1, B:] = e[:, 128:]
            return carry

        for i in range(ITERS):
            if i == 0:
                send(F.at[0], F.at[NX], G0, mate)
                arrived(CR, UP)
                XS[0] = CS[...] + CR[...]
            for k in range(1, NX):
                send(XS.at[i], XR.at[i, k - 1], XX + i, dev(k, 0, 0, 0))
            if i == 0:
                arrived(F.at[NX], G0)
                lax.fori_loop(0, CH, mate_exp, 0, unroll=4)
            elif i == 1:
                blocks(0, 1)
                blocks(NX, NX + 1)
            else:
                arrived(F.at[pl.ds(NX + 1, NX - 1)], G2)
                blocks(NX + 1, 2 * NX)
            arrived(XR.at[i], XX + i)
            YS[i] = (XS[i] + XR[i, 0]) + (XR[i, 1] + XR[i, 2])
            for k in range(1, NY):
                send(YS.at[i], YR.at[i, k - 1], YY + i, dev(0, k, 0, 0))
            if i == 0:
                gather_x()
                student()
            elif i == 1:
                hand_totals()
                hand_blocks()
                blocks(1, NX)
            else:
                line_totals()
            arrived(YR.at[i], YY + i)
            total = YS[i]
            for k in range(NY - 1):
                total = total + YR[i, k]
            CF[i] = 1.0 / total
            if i == last:
                send(CF.at[last], CF.at[last], DN, mate)

            def step(t, acc):
                return acc + E[t] * CF[i, pl.ds(t, 1), :]

            acc = lax.fori_loop(0, TL, step, jnp.zeros((2 * B, 128), jnp.float32), unroll=4)
            ZS[i, 0:1, :] = jnp.sum(acc[:B].T, 0, keepdims=True)
            ZS[i, 1:2, :] = jnp.sum(acc[B:].T, 0, keepdims=True)
            if i < last:
                for k in range(1, NZ):
                    send(ZS.at[i], ZRV.at[i, k - 1], ZZ + i, dev(0, 0, 0, k))
                if i == 0:
                    student_totals()
                arrived(ZRV.at[i], ZZ + i)
                total = ZS[i]
                for k in range(NZ - 1):
                    total = total + ZRV[i, k]
                inv = 1.0 / total
                RW[:B] = across(inv[0:1])
                RW[B:] = across(inv[1:2])

                def scaled(t, carry):
                    e = E[t] * RW[...]
                    XS[i + 1, pl.ds(t, 1), :] = jnp.sum(e[:B] + e[B:], 0, keepdims=True)
                    return carry

                lax.fori_loop(0, TL, scaled, 0, unroll=4)
            else:
                for k in range(1, NX * NZ):
                    send(ZS.at[i], ZL.at[k], ZZ + i, dev(k // NZ, 0, 0, k % NZ))
                ZL[0] = ZS[i]
                arrived(ZL.at[pl.ds(1, NX * NZ - 1)], ZZ + i)
                for dx in range(NX):
                    total = ZL[dx * NZ]
                    for dz in range(1, NZ):
                        total = total + ZL[dx * NZ + dz]
                    inv = 1.0 / total
                    RB[dx] = inv[0:1]
                    RB[NX + dx] = inv[1:2]
                    RBM[dx] = inv[1:2]
                    RBM[NX + dx] = inv[0:1]
                send(RBM, RB, RM, mate)

    first_tile = (x * NC + c) * (KB // 128)

    def line_grad(j, carry):
        rb = across(RB[j] * SCALE)
        for q in range(KB // 128):
            h, part = q // 2, pl.ds(128 * (q % 2), 128)
            col = CF[last, pl.ds(first_tile + q, 1), :]
            g = ESB[j, h, :, part] * ITB[j] - (ETB[j, h, :, part] * col) * rb
            GB[j, :, 128 * q:128 * q + 128] = g.astype(jnp.bfloat16)
        return carry

    lax.fori_loop(0, 2 * NX, line_grad, 0, unroll=2)
    for h in range(KB // 256):
        acc = jnp.zeros((D, 256), jnp.float32)
        for p in range(NX):
            lhs = jnp.concatenate([SBT[2 * p], SBT[2 * p + 1]], 1)
            rhs = jnp.concatenate(
                [GB[2 * p, :, 256 * h:256 * h + 256], GB[2 * p + 1, :, 256 * h:256 * h + 256]], 0
            )
            acc = acc + dot(lhs, rhs)
        GPS[:, :, 256 * h:256 * h + 256] = acc.reshape(D // 4, 4, 256)

    def scatter(i, carry):
        to = dev(i // (NY * NC), lax.rem(i // NC, NY), lax.rem(i, NC), 0)
        send(GPS.at[to[0]], GPR.at[i], GP, to)
        return carry

    lax.fori_loop(1, NX * NY * NC, scatter, 0)

    RW[:B] = across(RB[0] * SCALE)

    def feature(j, acc):
        g = [
            (SE[2 * j + h] * ITW[...] - (E[2 * j + h, :B] * CF[last, pl.ds(2 * j + h, 1), :]) * RW[:B]).astype(jnp.bfloat16)
            for h in range(2)
        ]
        return acc + lax.dot_general(
            jnp.concatenate(g, 1), WU[j], (((1,), (1,)), ((), ())), preferred_element_type=jnp.float32
        )

    GFA[...] = lax.fori_loop(0, CH, feature, jnp.zeros((B, D), jnp.float32), unroll=4)
    for k in range(NZ):
        GFS[k] = GFA[16 * k:16 * k + 16, :]
    for k in range(1, NZ):
        send(GFS.at[lax.rem(z + k, NZ)], GFR.at[k - 1], ZR, dev(0, 0, 0, k))

    arrived(GFR, ZR)
    mine = pl.ds(pl.multiple_of(z * 16, 16), 16)
    u, inv = unit_rows(s_ref[mine, :])
    u = u.astype(jnp.float32)
    total = GFS[z]
    for k in range(NZ - 1):
        total = total + GFR[k]
    GFO[0] = (total - u * jnp.sum(u * total, 1, keepdims=True)) * inv
    for k in range(1, NZ):
        send(GFO.at[0], GFO.at[k], ZA, dev(0, 0, 0, k))
    gf_out[mine, :] = GFO[0]

    arrived(GPR.at[pl.ds(1, NX * NY * NC - 1)], GP)
    GPR[0] = GPS[dp]
    for dx in range(NX):
        for dc in range(NC):
            total = GPR[dx * NY * NC + dc]
            for dy in range(1, NY):
                total = total + GPR[(dx * NY + dy) * NC + dc]
            at = (lax.rem(x + NX - dx, NX) * NC + lax.rem(c + dc, NC)) * KB
            gp_out[:, pl.ds(pl.multiple_of(at, KB), KB)] = total

    arrived(GFO.at[pl.ds(1, NZ - 1)], ZA)
    for k in range(1, NZ):
        at = lax.rem(z + NZ - k, NZ) * 16
        gf_out[pl.ds(pl.multiple_of(at, 16), 16), :] = GFO[k]

    @pl.when(c == 0)
    def _():
        sent(CS, UP)

    @pl.when(c == 1)
    def _():
        for i in range(ITERS):
            sent(XR.at[i], XX + i)
            sent(YR.at[i], YY + i)
            if i < last:
                sent(ZRV.at[i], ZZ + i)
        sent(ZL.at[pl.ds(1, NX * NZ - 1)], ZZ + last)
        sent(CF.at[last], DN)
        sent(RBM, RM)

    sent(TZR, TZ)
    sent(F.at[0], G0)
    sent(F.at[pl.ds(1, NX - 1)], G1)
    sent(F.at[pl.ds(1, NX - 1)], G2)
    sent(TS.at[pl.ds(1, NX - 1)], T1)
    sent(TS.at[pl.ds(0, NX)], T2)
    sent(GPR.at[pl.ds(1, NX * NY * NC - 1)], GP)
    sent(GFR, ZR)
    sent(GFO.at[pl.ds(1, NZ - 1)], ZA)


def shards(teacher, student, protos):
    f32, bf16 = jnp.float32, jnp.bfloat16
    vm = pltpu.VMEM
    scratch = [
        vm((B, D), bf16),
        vm((B, D), bf16),
        vm((D, K), bf16),
        vm((CH, D, 256), bf16),
        vm((TL, 2 * B, 128), f32),
        vm((TL, B, 128), f32),
        vm((2 * NX, 2 * B, D), f32),
        vm((2 * NX, KB // 256, B, 256), f32),
        vm((2 * NX, KB // 256, B, 256), f32),
        vm((2 * NX, D, B), bf16),
        vm((2 * NX, B, KB), bf16),
        vm((64, 4, KB), f32),
        vm((64, 4, KB), f32),
        vm((NZ, 16, D), f32),
        vm((NZ - 1, 16, D), f32),
        vm((NZ, 16, D), f32),
        vm((B, D), f32),
        vm((TL, 128), f32),
        vm((TL, 128), f32),
        vm((ITERS, TL, 128), f32),
        vm((ITERS, NX - 1, TL, 128), f32),
        vm((ITERS, TL, 128), f32),
        vm((ITERS, NY - 1, TL, 128), f32),
        vm((ITERS, TL, 128), f32),
        vm((ITERS, 2, 128), f32),
        vm((ITERS - 1, NZ - 1, 2, 128), f32),
        vm((NX * NZ, 2, 128), f32),
        vm((1, 128), f32),
        vm((NZ - 1, 1, 128), f32),
        vm((2 * NX, 1, 128), f32),
        vm((2 * NX, 1, 128), f32),
        vm((2 * NX, 1, 128), f32),
        vm((2 * NX, B, 128), f32),
        vm((2 * B, 128), f32),
        vm((B, 128), f32),
        pltpu.SemaphoreType.DMA((2 + LOADS,)),
        pltpu.SemaphoreType.DMA((GROUPS,)),
        pltpu.SemaphoreType.DMA((GROUPS,)),
    ]
    whole = pl.BlockSpec(memory_space=pltpu.VMEM)
    anywhere = pl.BlockSpec(memory_space=pl.ANY)
    return pl.pallas_call(
        body,
        out_shape=(jax.ShapeDtypeStruct((B, D), f32), jax.ShapeDtypeStruct((4, K), f32)),
        in_specs=[anywhere] * 3,
        out_specs=(whole, whole),
        scratch_shapes=scratch,
        compiler_params=pltpu.CompilerParams(
            collective_id=0, has_side_effects=True, vmem_limit_bytes=60 * 2**20
        ),
    )(teacher, student, protos)


def solution(mesh):
    placed = (P("dp", None), P("dp", None), P(None, "proto"))
    return jax.shard_map(
        shards,
        mesh=mesh,
        in_specs=placed,
        out_specs=(P("dp", None), P("dp", "proto")),
        check_vma=False,
    )
```

time: 87.6 us -> 77.3 us (0.88)
  Pallas kernels: 82.2 us -> 73.4 us
  local copies, waits for them, and re-layouts: 4.55 us -> 3.04 us
    pallas_call x1, Pallas kernels: 82.2 us -> 73.4 us  [shards(): pl.pallas_call(body, out_shape=(jax.ShapeDtypeStruct((B, D), f32), jax.Sh...]
    unnamed x8 -> x2, local copies, waits for them, and re-layouts: 4.55 us -> 3.04 us
where the time goes in v2:
time: 77.3 us; the launch traced here: 77.1 us
  Pallas kernels  73.4 us (95%)
  local copies, waits for them, and re-layouts  3.04 us (4%)
    pallas_call x1, Pallas kernels, shards(): pl.pallas_call(body, out_shape=(jax.ShapeDtypeStruct((B, D), f32), jax.Sh...  73.4 us
    unnamed x2, local copies, waits for them, and re-layouts  3.04 us

profile of v2, /device:TPU:1, one launch (start us, length us, event | category | flops | bytes accessed | tf_op | source)
XLA Modules:
  0.0 77.1 jit_solution(6557726388594743091)
XLA Ops:
  0.6 73.4 %shard_map.50 = (f32[128,256]{1,0:T(8,128)}, f32[4,4096]{1,0:T(4,128)}) custom-call(bf16[128,256]{1,0:T(8,128)(2,1)} %t_hbm.1, bf16[128,256]{1,0:T(8,128)(2,1)} %s_hbm.1, bf16[256,4096]{1,0:T(8,128)(2,1)} %w_hbm.1), custom_call_target="tpu_custom_call" | custom-call | tf_op jit(solution)/shard_map/pallas_call | solution.py:426
  74.0 1.6 %copy.7 = f32[128,256]{1,0:T(8,128)} copy(f32[128,256]{1,0:T(8,128)} %get-tuple-element.4) | data formatting | bytes 262144
  75.6 1.5 %copy.8 = f32[4,4096]{1,0:T(4,128)} copy(f32[4,4096]{1,0:T(4,128)} %get-tuple-element.5) | data formatting | bytes 131072

commit v3 on v2

v3 whole, which is shorter than its diff:
```python
import functools

import jax
import jax.numpy as jnp
from jax import lax
from jax.experimental import pallas as pl
from jax.experimental.pallas import tpu as pltpu
from jax.sharding import PartitionSpec as P

EPS = 1e-06
INV_T = 1.0 / 0.07
INV_S = 1.0 / 0.1
ITERS = 3
NX, NY, NC, NZ = 4, 8, 2, 8
B = 128
D = 256
K = 4096
CH = K // 256
TL = K // 128
NB = 2 * NX
KB = K // (NB * NC)
SCALE = 32768 / 64.0 / 0.1
MESH = pl.DeviceIdType.MESH

UP, DN, G0, GY, G1, G2, TZ, T1, T2, RM, GP, AR, TR, ZA = range(14)
XX, YY, ZZ = (14, 17, 20)
GROUPS = 23
XO = (2, 1, 3)
YO = ZO = (4, 3, 5, 2, 6, 1, 7)
LOADS = 4


def dot(a, b):
    return jnp.dot(a, b, preferred_element_type=jnp.float32)


def unit_rows(raw):
    wide = raw.astype(jnp.float32)
    inv = lax.rsqrt(jnp.sum(wide * wide, 1, keepdims=True) + EPS)
    return (wide * inv).astype(jnp.bfloat16), inv


def across(row):
    return jnp.broadcast_to(row, (128, 128)).T


def body(
    t_hbm, s_hbm, w_hbm, gf_out, gp_out,
    t_ref, s_ref, w_ref, WU, E, SE, F, ETB, ESB, SBT, GB, GPS, GPR, GAS, GAR, GTS, GTR, GFO, GFA,
    CS, CR, XS, XR, YS, YR, CF, ZS, ZRV, ZL, TZS, TZR, TS, RB, RBM, ITB, RW, ITW, lsem, ssem, rsem,
):
    dp = lax.axis_index("dp")
    z = lax.axis_index("proto")
    c = lax.rem(dp, 2)
    y = lax.rem(dp // 2, NY)
    x = dp // (2 * NY)

    def dev(dx, dy, dc, dz):
        return (
            (lax.rem(x + dx, NX) * NY + lax.rem(y + dy, NY)) * NC + lax.rem(c + dc, NC),
            lax.rem(z + dz, NZ),
        )

    mate = dev(0, 0, 1, 0)
    flip = NY + 1 - 2 * lax.rem(y, 2)

    def send(src, dst, group, to):
        pltpu.make_async_remote_copy(
            src, dst, ssem.at[group], rsem.at[group], device_id=to, device_id_type=MESH
        ).start()

    def arrived(ref, group):
        pltpu.make_async_remote_copy(
            ref, ref, ssem.at[group], rsem.at[group], device_id=mate, device_id_type=MESH
        ).wait_recv()

    def sent(ref, group):
        pltpu.make_async_remote_copy(
            ref, ref, ssem.at[group], rsem.at[group], device_id=mate, device_id_type=MESH
        ).wait_send()

    loads = [
        pltpu.make_async_copy(t_hbm, t_ref, lsem.at[0]),
        pltpu.make_async_copy(s_hbm, s_ref, lsem.at[1]),
    ]
    for piece in range(LOADS):
        cols = pl.ds(piece * (K // LOADS), K // LOADS)
        loads.append(pltpu.make_async_copy(w_hbm.at[:, cols], w_ref.at[:, cols], lsem.at[2 + piece]))
    for load in loads:
        load.start()

    peers = [dev(0, 0, 1, 0)]
    peers += [dev(k, 0, 0, 0) for k in range(1, NX)]
    peers += [dev(0, k, 0, 0) for k in range(1, NY)]
    peers += [dev(0, 0, 0, k) for k in range(1, NZ)]
    peers += [dev(k, flip, 0, 0) for k in range(1, NX)]
    barrier = pltpu.get_barrier_semaphore()
    for to in peers:
        pl.semaphore_signal(barrier, inc=1, device_id=to, device_id_type=MESH)

    loads[0].wait()
    t_unit, _ = unit_rows(t_ref[...])
    F[0, :B, :] = t_unit.astype(jnp.float32)

    def first(j, carry):
        w = w_ref[:, pl.ds(pl.multiple_of(j * 256, 256), 256)].astype(jnp.float32)
        w = (w * lax.rsqrt(jnp.sum(w * w, 0, keepdims=True) + EPS)).astype(jnp.bfloat16)
        WU[j] = w
        e = jnp.exp(dot(t_unit, w) * INV_T)
        E[2 * j, :B] = e[:, :128]
        E[2 * j + 1, :B] = e[:, 128:]
        CS[pl.ds(2 * j, 1), :] = jnp.sum(e[:, :128], 0, keepdims=True)
        CS[pl.ds(2 * j + 1, 1), :] = jnp.sum(e[:, 128:], 0, keepdims=True)
        return carry

    per = CH // LOADS
    for piece in range(LOADS):
        loads[2 + piece].wait()
        lax.fori_loop(piece * per, piece * per + per, first, 0, unroll=True)
    loads[1].wait()
    s_unit, _ = unit_rows(s_ref[...])
    F[0, B:, :] = s_unit.astype(jnp.float32)
    pl.semaphore_wait(barrier, len(peers))

    def student():
        def step(j, acc):
            e = jnp.exp(dot(F[0, B:, :].astype(jnp.bfloat16), WU[j]) * INV_S)
            SE[2 * j] = e[:, :128]
            SE[2 * j + 1] = e[:, 128:]
            return acc + e[:, :128] + e[:, 128:]

        acc = lax.fori_loop(0, CH, step, jnp.zeros((B, 128), jnp.float32), unroll=4)
        TZS[...] = jnp.sum(acc.T, 0, keepdims=True)
        for k in ZO:
            send(TZS, TZR.at[k - 1], TZ, dev(0, 0, 0, k))

    def product(tile, kept, got, group):
        def step(j, acc):
            g = jnp.concatenate([tile(2 * j), tile(2 * j + 1)], 1)
            high = g.astype(jnp.bfloat16)
            low = (g - high.astype(jnp.float32)).astype(jnp.bfloat16)
            return acc + lax.dot_general(
                jnp.concatenate([high, low], 0), WU[j], (((1,), (1,)), ((), ())), preferred_element_type=jnp.float32
            )

        acc = lax.fori_loop(0, CH, step, jnp.zeros((2 * B, D), jnp.float32), unroll=2)
        GFA[...] = acc[:B] + acc[B:]
        for k in range(NZ):
            kept[k] = GFA[16 * k:16 * k + 16, :]
        for k in ZO:
            send(kept.at[lax.rem(z + k, NZ)], got.at[k - 1], group, dev(0, 0, 0, k))

    def student_product():
        product(lambda t: SE[t] * ITW[...], GAS, GAR, AR)

    def teacher_product():
        product(lambda t: E[t, :B] * CF[ITERS - 1, pl.ds(t, 1), :], GTS, GTR, TR)

    def student_totals():
        arrived(TZR, TZ)
        total = TZS[...]
        for k in range(NZ - 1):
            total = total + TZR[k]
        TS[0] = SCALE / total
        ITW[...] = across(TS[0])
        for k in XO:
            for p in (1, 0):
                send(TS.at[0], TS.at[2 * k + p], T1, dev(k, flip * p, 0, 0))
        send(TS.at[0], TS.at[1], T1, dev(0, flip, 0, 0))

    def hand_totals():
        arrived(TS.at[pl.ds(1, NB - 1)], T1)
        send(TS.at[pl.ds(0, NB)], TS.at[pl.ds(NB, NB)], T2, mate)

    def line_totals():
        arrived(TS.at[pl.ds(NB, NB)], T2)
        for j in range(2 * NB):
            ITB[j] = across(TS[j])

    def gather_y():
        send(F.at[0], F.at[1], GY, dev(0, flip, 0, 0))

    def gather_x():
        arrived(F.at[1], GY)
        for k in XO:
            send(F.at[pl.ds(0, 2)], F.at[pl.ds(2 * k, 2)], G1, dev(k, 0, 0, 0))

    def hand_blocks():
        arrived(F.at[pl.ds(2, NB - 2)], G1)
        send(F.at[pl.ds(1, NB - 1)], F.at[pl.ds(NB + 1, NB - 1)], G2, mate)

    own = (x * 2 + lax.rem(y, 2)) * NC + c

    def line_block(j, carry):
        tb = F[j, :B, :].astype(jnp.bfloat16)
        sw = F[j, B:, :]
        SBT[j] = sw.T.astype(jnp.bfloat16)
        ETB[j] = jnp.exp(dot(tb, WU[own]) * INV_T)
        ESB[j] = jnp.exp(dot(sw.astype(jnp.bfloat16), WU[own]) * INV_S)
        return carry

    def blocks(lo, hi):
        lax.fori_loop(lo, hi, line_block, 0)

    last = ITERS - 1

    @pl.when(c == 0)
    def _():
        send(CS, CR, UP, mate)
        send(F.at[0], F.at[NB], G0, mate)
        gather_y()
        student()
        blocks(0, 1)
        student_totals()
        arrived(F.at[NB], G0)
        gather_x()
        blocks(NB, NB + 1)
        student_product()
        blocks(1, 2)
        hand_totals()
        line_totals()
        hand_blocks()
        blocks(2, NB)
        arrived(F.at[pl.ds(NB + 1, NB - 1)], G2)
        blocks(NB + 1, 2 * NB)
        arrived(CF.at[last], DN)
        teacher_product()
        arrived(RB, RM)

    @pl.when(c == 1)
    def _():
        def mate_exp(j, carry):
            e = jnp.exp(dot(F[NB, :B, :].astype(jnp.bfloat16), WU[j]) * INV_T)
            E[2 * j, B:] = e[:, :128]
            E[2 * j + 1, B:] = e[:, 128:]
            return carry

        for i in range(ITERS):
            if i == 0:
                send(F.at[0], F.at[NB], G0, mate)
                arrived(CR, UP)
                XS[0] = CS[...] + CR[...]
            for k in XO:
                send(XS.at[i], XR.at[i, k - 1], XX + i, dev(k, 0, 0, 0))
            if i == 0:
                gather_y()
                arrived(F.at[NB], G0)
                lax.fori_loop(0, CH, mate_exp, 0, unroll=4)
            elif i == 1:
                blocks(0, 2)
                blocks(NB, NB + 1)
                hand_totals()
            arrived(XR.at[i], XX + i)
            YS[i] = (XS[i] + XR[i, 0]) + (XR[i, 1] + XR[i, 2])
            for k in YO:
                send(YS.at[i], YR.at[i, k - 1], YY + i, dev(0, k, 0, 0))
            if i == 0:
                student()
            elif i == 1:
                student_product()
            else:
                hand_blocks()
                blocks(2, NB)
            arrived(YR.at[i], YY + i)
            total = YS[i]
            for k in range(NY - 1):
                total = total + YR[i, k]
            CF[i] = 1.0 / total
            if i == last:
                send(CF.at[last], CF.at[last], DN, mate)

            def step(t, acc):
                return acc + E[t] * CF[i, pl.ds(t, 1), :]

            acc = lax.fori_loop(0, TL, step, jnp.zeros((2 * B, 128), jnp.float32), unroll=4)
            ZS[i, 0:1, :] = jnp.sum(acc[:B].T, 0, keepdims=True)
            ZS[i, 1:2, :] = jnp.sum(acc[B:].T, 0, keepdims=True)
            if i < last:
                for k in ZO:
                    send(ZS.at[i], ZRV.at[i, k - 1], ZZ + i, dev(0, 0, 0, k))
                if i == 0:
                    student_totals()
                    gather_x()
                else:
                    line_totals()
                arrived(ZRV.at[i], ZZ + i)
                total = ZS[i]
                for k in range(NZ - 1):
                    total = total + ZRV[i, k]
                inv = 1.0 / total
                RW[:B] = across(inv[0:1])
                RW[B:] = across(inv[1:2])

                def scaled(t, carry):
                    e = E[t] * RW[...]
                    XS[i + 1, pl.ds(t, 1), :] = jnp.sum(e[:B] + e[B:], 0, keepdims=True)
                    return carry

                lax.fori_loop(0, TL, scaled, 0, unroll=4)
            else:
                far = lambda k: -(min(k // (2 * NZ), NX - k // (2 * NZ)) + k // NZ % 2 + min(k % NZ, NZ - k % NZ))
                for k in sorted(range(1, NB * NZ), key=far):
                    to = dev(k // (2 * NZ), flip * (k // NZ % 2), 0, k % NZ)
                    send(ZS.at[i], ZL.at[k], ZZ + i, to)
                ZL[0] = ZS[i]
                teacher_product()
                arrived(F.at[pl.ds(NB + 1, NB - 1)], G2)
                blocks(NB + 1, 2 * NB)
                arrived(ZL.at[pl.ds(1, NB * NZ - 1)], ZZ + i)
                for j in range(NB):
                    total = ZL[j * NZ]
                    for dz in range(1, NZ):
                        total = total + ZL[j * NZ + dz]
                    inv = 1.0 / total
                    RB[j] = inv[0:1]
                    RB[NB + j] = inv[1:2]
                    RBM[j] = inv[1:2]
                    RBM[NB + j] = inv[0:1]
                send(RBM, RB, RM, mate)

    def line_grad(j, carry):
        rb = across(RB[j] * SCALE)
        for q in range(KB // 128):
            part = pl.ds(128 * q, 128)
            col = CF[last, pl.ds(own * (KB // 128) + q, 1), :]
            g = ESB[j, :, part] * ITB[j] - (ETB[j, :, part] * col) * rb
            GB[j, :, 128 * q:128 * q + 128] = g.astype(jnp.bfloat16)
        return carry

    lax.fori_loop(0, 2 * NB, line_grad, 0, unroll=4)
    acc = jnp.zeros((D, KB), jnp.float32)
    for p in range(NB):
        lhs = jnp.concatenate([SBT[2 * p], SBT[2 * p + 1]], 1)
        acc = acc + dot(lhs, jnp.concatenate([GB[2 * p], GB[2 * p + 1]], 0))
    GPS[...] = acc.reshape(D // 4, 4, KB)

    for dy in YO + (0,):
        def scatter(i, carry):
            to = dev(i // NC, dy, lax.rem(i, NC), 0)
            send(GPS.at[to[0]], GPR.at[i // NC * (NY * NC) + dy * NC + lax.rem(i, NC)], GP, to)
            return carry

        lax.fori_loop(0 if dy else 1, NX * NC, scatter, 0)

    RW[:B] = across(RB[0] * SCALE)
    mine = pl.ds(pl.multiple_of(z * 16, 16), 16)
    u, inv = unit_rows(s_ref[mine, :])
    u = u.astype(jnp.float32)
    arrived(GAR, AR)
    arrived(GTR, TR)
    total, teach = GAS[z], GTS[z]
    for k in range(NZ - 1):
        total = total + GAR[k]
        teach = teach + GTR[k]
    total = total - teach * RW[mine, 0:1]
    GFO[0] = (total - u * jnp.sum(u * total, 1, keepdims=True)) * inv
    for k in ZO:
        send(GFO.at[0], GFO.at[k], ZA, dev(0, 0, 0, k))
    gf_out[mine, :] = GFO[0]
    arrived(GFO.at[pl.ds(1, NZ - 1)], ZA)
    for k in range(1, NZ):
        at = lax.rem(z + NZ - k, NZ) * 16
        gf_out[pl.ds(pl.multiple_of(at, 16), 16), :] = GFO[k]

    arrived(GPR.at[pl.ds(1, NX * NY * NC - 1)], GP)
    GPR[0] = GPS[dp]
    for dx in range(NX):
        for dc in range(NC):
            for p in range(2):
                total = GPR[(dx * NY + p) * NC + dc]
                for dy in range(p + 2, NY, 2):
                    total = total + GPR[(dx * NY + dy) * NC + dc]
                at = (lax.rem(x + NX - dx, NX) * 2 + lax.rem(y + p, 2)) * NC + lax.rem(c + dc, NC)
                gp_out[:, pl.ds(pl.multiple_of(at * KB, KB), KB)] = total

    @pl.when(c == 0)
    def _():
        sent(CS, UP)

    @pl.when(c == 1)
    def _():
        for i in range(ITERS):
            sent(XR.at[i], XX + i)
            sent(YR.at[i], YY + i)
            if i < last:
                sent(ZRV.at[i], ZZ + i)
        sent(ZL.at[pl.ds(1, NB * NZ - 1)], ZZ + last)
        sent(CF.at[last], DN)
        sent(RBM, RM)

    sent(TZR, TZ)
    sent(F.at[0], G0)
    sent(F.at[0], GY)
    sent(F.at[pl.ds(2, NB - 2)], G1)
    sent(F.at[pl.ds(1, NB - 1)], G2)
    sent(TS.at[pl.ds(1, NB - 1)], T1)
    sent(TS.at[pl.ds(0, NB)], T2)
    sent(GPR.at[pl.ds(1, NX * NY * NC - 1)], GP)
    sent(GAR, AR)
    sent(GTR, TR)
    sent(GFO.at[pl.ds(1, NZ - 1)], ZA)


def place(features, protos, features_out, protos_out, sem):
    copies = [
        pltpu.make_async_copy(features, features_out, sem.at[0]),
        pltpu.make_async_copy(protos, protos_out, sem.at[1]),
    ]
    for copy in copies:
        copy.start()
    for copy in copies:
        copy.wait()


def shards(teacher, student, protos):
    f32, bf16 = jnp.float32, jnp.bfloat16
    vm = pltpu.VMEM
    scratch = [
        vm((B, D), bf16),
        vm((B, D), bf16),
        vm((D, K), bf16),
        vm((CH, D, 256), bf16),
        vm((TL, 2 * B, 128), f32),
        vm((TL, B, 128), f32),
        vm((2 * NB, 2 * B, D), f32),
        vm((2 * NB, B, KB), f32),
        vm((2 * NB, B, KB), f32),
        vm((2 * NB, D, B), bf16),
        vm((2 * NB, B, KB), bf16),
        vm((64, 4, KB), f32),
        vm((64, 4, KB), f32),
        vm((NZ, 16, D), f32),
        vm((NZ - 1, 16, D), f32),
        vm((NZ, 16, D), f32),
        vm((NZ - 1, 16, D), f32),
        vm((NZ, 16, D), f32),
        vm((B, D), f32),
        vm((TL, 128), f32),
        vm((TL, 128), f32),
        vm((ITERS, TL, 128), f32),
        vm((ITERS, NX - 1, TL, 128), f32),
        vm((ITERS, TL, 128), f32),
        vm((ITERS, NY - 1, TL, 128), f32),
        vm((ITERS, TL, 128), f32),
        vm((ITERS, 2, 128), f32),
        vm((ITERS - 1, NZ - 1, 2, 128), f32),
        vm((NB * NZ, 2, 128), f32),
        vm((1, 128), f32),
        vm((NZ - 1, 1, 128), f32),
        vm((2 * NB, 1, 128), f32),
        vm((2 * NB, 1, 128), f32),
        vm((2 * NB, 1, 128), f32),
        vm((2 * NB, B, 128), f32),
        vm((2 * B, 128), f32),
        vm((B, 128), f32),
        pltpu.SemaphoreType.DMA((2 + LOADS,)),
        pltpu.SemaphoreType.DMA((GROUPS,)),
        pltpu.SemaphoreType.DMA((GROUPS,)),
    ]
    whole = pl.BlockSpec(memory_space=pltpu.VMEM)
    anywhere = pl.BlockSpec(memory_space=pl.ANY)
    grads = pl.pallas_call(
        body,
        out_shape=(jax.ShapeDtypeStruct((B, D), f32), jax.ShapeDtypeStruct((4, K), f32)),
        in_specs=[anywhere] * 3,
        out_specs=(whole, whole),
        scratch_shapes=scratch,
        compiler_params=pltpu.CompilerParams(
            collective_id=0, has_side_effects=True, vmem_limit_bytes=60 * 2**20
        ),
    )(teacher, student, protos)
    return pl.pallas_call(
        place,
        out_shape=tuple(jax.ShapeDtypeStruct(g.shape, g.dtype) for g in grads),
        in_specs=[anywhere] * 2,
        out_specs=(anywhere,) * 2,
        scratch_shapes=[pltpu.SemaphoreType.DMA((2,))],
        compiler_params=pltpu.CompilerParams(vmem_limit_bytes=60 * 2**20),
    )(*grads)


def solution(mesh):
    placed = (P("dp", None), P("dp", None), P(None, "proto"))
    return jax.shard_map(
        shards,
        mesh=mesh,
        in_specs=placed,
        out_specs=(P("dp", None), P("dp", "proto")),
        check_vma=False,
    )
```

time: 77.3 us -> 89.9 us (1.16)
  Pallas kernels: 73.4 us -> 89.1 us
  local copies, waits for them, and re-layouts: 3.04 us -> 0 us
    pallas_call x1, Pallas kernels: 73.4 us -> 82 us  [shards(): pl.pallas_call(body, out_shape=(jax.ShapeDtypeStruct((B, D), f32), jax.Sh...]
    pallas_call x0 -> x1, Pallas kernels: none -> 7.08 us  [shards(): pl.pallas_call(place, out_shape=tuple((jax.ShapeDtypeStruct(g.shape, g.dt...]
    unnamed x2 -> x0, local copies, waits for them, and re-layouts: 3.04 us -> none
where the time goes in v3:
time: 89.9 us; the launch traced here: 89.7 us
  Pallas kernels  89.1 us (99%)
    pallas_call x1, Pallas kernels, shards(): pl.pallas_call(body, out_shape=(jax.ShapeDtypeStruct((B, D), f32), jax.Sh...  82 us
    pallas_call x1, Pallas kernels, shards(): pl.pallas_call(place, out_shape=tuple((jax.ShapeDtypeStruct(g.shape, g.dt...  7.08 us

profile of v3, /device:TPU:1, one launch (start us, length us, event | category | flops | bytes accessed | tf_op | source)
XLA Modules:
  0.0 89.7 jit_solution(18050433432957531994)
XLA Ops:
  0.6 82.0 %shard_map.50 = (f32[128,256]{1,0:T(8,128)}, f32[4,4096]{1,0:T(4,128)}) custom-call(bf16[128,256]{1,0:T(8,128)(2,1)} %t_hbm.1, bf16[128,256]{1,0:T(8,128)(2,1)} %s_hbm.1, bf16[256,4096]{1,0:T(8,128)(2,1)} %w_hbm.1), custom_call_target="tpu_custom_call" | custom-call | tf_op jit(solution)/shard_map/pallas_call | solution.py:462
  82.6 7.1 %shard_map.51 = (f32[128,256]{1,0:T(8,128)}, f32[4,4096]{1,0:T(4,128)}) custom-call(f32[128,256]{1,0:T(8,128)} %get-tuple-element.4.features, f32[4,4096]{1,0:T(4,128)} %get-tuple-element.5.protos), custom_call_target="tpu_custom_call" | custom-call | tf_op jit(solution)/shard_map/pallas_call | solution.py:472

commit v4 on v3

--- a/solution.py
+++ b/solution.py
@@ -22,9 +22,10 @@
 SCALE = 32768 / 64.0 / 0.1
 MESH = pl.DeviceIdType.MESH
 
-UP, DN, G0, GY, G1, G2, TZ, T1, T2, RM, GP, AR, TR, ZA = range(14)
-XX, YY, ZZ = (14, 17, 20)
-GROUPS = 23
+UP, DN, G0, GY, G2, TZ, T1, T2, RM, GP, AR, TR, ZA = range(13)
+XX, YY, ZZ = (13, 16, 19)
+GL, GR, GF = (22, 24, 26)
+GROUPS = 28
 XO = (2, 1, 3)
 YO = ZO = (4, 3, 5, 2, 6, 1, 7)
 LOADS = 4
@@ -177,16 +178,31 @@
         for j in range(2 * NB):
             ITB[j] = across(TS[j])
 
-    def gather_y():
+    def to_sides(p):
+        send(F.at[p], F.at[2 + p], GL + p, dev(1, 0, 0, 0))
+        send(F.at[p], F.at[6 + p], GR + p, dev(3, 0, 0, 0))
+
+    def relay(p):
+        arrived(F.at[2 + p], GL + p)
+        arrived(F.at[6 + p], GR + p)
+        send(F.at[2 + p, pl.ds(0, B)], F.at[4 + p, pl.ds(0, B)], GF + p, dev(1, 0, 0, 0))
+        send(F.at[6 + p, pl.ds(B, B)], F.at[4 + p, pl.ds(B, B)], GF + p, dev(3, 0, 0, 0))
+
+    def gather_1():
         send(F.at[0], F.at[1], GY, dev(0, flip, 0, 0))
-
-    def gather_x():
+        to_sides(0)
+
+    def gather_2():
         arrived(F.at[1], GY)
-        for k in XO:
-            send(F.at[pl.ds(0, 2)], F.at[pl.ds(2 * k, 2)], G1, dev(k, 0, 0, 0))
-
-    def hand_blocks():
-        arrived(F.at[pl.ds(2, NB - 2)], G1)
+        to_sides(1)
+        relay(0)
+
+    def gather_3():
+        relay(1)
+
+    def gather_4():
+        for p in range(2):
+            arrived(F.at[4 + p], GF + p)
         send(F.at[pl.ds(1, NB - 1)], F.at[pl.ds(NB + 1, NB - 1)], G2, mate)
 
     own = (x * 2 + lax.rem(y, 2)) * NC + c
@@ -208,18 +224,19 @@
     def _():
         send(CS, CR, UP, mate)
         send(F.at[0], F.at[NB], G0, mate)
-        gather_y()
+        gather_1()
         student()
         blocks(0, 1)
         student_totals()
         arrived(F.at[NB], G0)
-        gather_x()
+        gather_2()
         blocks(NB, NB + 1)
+        blocks(1, 2)
+        gather_3()
+        hand_totals()
         student_product()
-        blocks(1, 2)
-        hand_totals()
         line_totals()
-        hand_blocks()
+        gather_4()
         blocks(2, NB)
         arrived(F.at[pl.ds(NB + 1, NB - 1)], G2)
         blocks(NB + 1, 2 * NB)
@@ -243,13 +260,15 @@
             for k in XO:
                 send(XS.at[i], XR.at[i, k - 1], XX + i, dev(k, 0, 0, 0))
             if i == 0:
-                gather_y()
+                gather_1()
                 arrived(F.at[NB], G0)
                 lax.fori_loop(0, CH, mate_exp, 0, unroll=4)
             elif i == 1:
                 blocks(0, 2)
                 blocks(NB, NB + 1)
                 hand_totals()
+            else:
+                blocks(2, NB)
             arrived(XR.at[i], XX + i)
             YS[i] = (XS[i] + XR[i, 0]) + (XR[i, 1] + XR[i, 2])
             for k in YO:
@@ -257,10 +276,11 @@
             if i == 0:
                 student()
             elif i == 1:
+                gather_3()
                 student_product()
             else:
-                hand_blocks()
-                blocks(2, NB)
+                arrived(F.at[pl.ds(NB + 1, NB - 1)], G2)
+                blocks(NB + 1, 2 * NB)
             arrived(YR.at[i], YY + i)
             total = YS[i]
             for k in range(NY - 1):
@@ -280,8 +300,9 @@
                     send(ZS.at[i], ZRV.at[i, k - 1], ZZ + i, dev(0, 0, 0, k))
                 if i == 0:
                     student_totals()
-                    gather_x()
+                    gather_2()
                 else:
+                    gather_4()
                     line_totals()
                 arrived(ZRV.at[i], ZZ + i)
                 total = ZS[i]
@@ -304,8 +325,6 @@
                     send(ZS.at[i], ZL.at[k], ZZ + i, to)
                 ZL[0] = ZS[i]
                 teacher_product()
-                arrived(F.at[pl.ds(NB + 1, NB - 1)], G2)
-                blocks(NB + 1, 2 * NB)
                 arrived(ZL.at[pl.ds(1, NB * NZ - 1)], ZZ + i)
                 for j in range(NB):
                     total = ZL[j * NZ]
@@ -391,7 +410,10 @@
     sent(TZR, TZ)
     sent(F.at[0], G0)
     sent(F.at[0], GY)
-    sent(F.at[pl.ds(2, NB - 2)], G1)
+    for p in range(2):
+        sent(F.at[p], GL + p)
+        sent(F.at[p], GR + p)
+        sent(F.at[4 + p], GF + p)
     sent(F.at[pl.ds(1, NB - 1)], G2)
     sent(TS.at[pl.ds(1, NB - 1)], T1)
     sent(TS.at[pl.ds(0, NB)], T2)
@@ -401,15 +423,9 @@
     sent(GFO.at[pl.ds(1, NZ - 1)], ZA)
 
 
-def place(features, protos, features_out, protos_out, sem):
-    copies = [
-        pltpu.make_async_copy(features, features_out, sem.at[0]),
-        pltpu.make_async_copy(protos, protos_out, sem.at[1]),
-    ]
-    for copy in copies:
-        copy.start()
-    for copy in copies:
-        copy.wait()
+def place(features, protos, features_out, protos_out):
+    features_out[...] = features[...]
+    protos_out[...] = protos[...]
 
 
 def shards(teacher, student, protos):
@@ -472,9 +488,8 @@
     return pl.pallas_call(
         place,
         out_shape=tuple(jax.ShapeDtypeStruct(g.shape, g.dtype) for g in grads),
-        in_specs=[anywhere] * 2,
-        out_specs=(anywhere,) * 2,
-        scratch_shapes=[pltpu.SemaphoreType.DMA((2,))],
+        in_specs=[whole] * 2,
+        out_specs=(whole,) * 2,
         compiler_params=pltpu.CompilerParams(vmem_limit_bytes=60 * 2**20),
     )(*grads)
 

time: 89.9 us -> 72.1 us (0.80)
  Pallas kernels: 89.1 us -> 71.3 us
    pallas_call x1, Pallas kernels: 82 us -> 69.7 us  [shards(): pl.pallas_call(body, out_shape=(jax.ShapeDtypeStruct((B, D), f32), jax.Sh...]
    pallas_call x1, Pallas kernels: 7.08 us -> 1.59 us  [shards(): pl.pallas_call(place, out_shape=tuple((jax.ShapeDtypeStruct(g.shape, g.dt...]
where the time goes in v4:
time: 72.1 us; the launch traced here: 71.9 us
  Pallas kernels  71.3 us (99%)
    pallas_call x1, Pallas kernels, shards(): pl.pallas_call(body, out_shape=(jax.ShapeDtypeStruct((B, D), f32), jax.Sh...  69.7 us
    pallas_call x1, Pallas kernels, shards(): pl.pallas_call(place, out_shape=tuple((jax.ShapeDtypeStruct(g.shape, g.dt...  1.59 us

profile of v4, /device:TPU:1, one launch (start us, length us, event | category | flops | bytes accessed | tf_op | source)
XLA Modules:
  0.0 71.9 jit_solution(15309204961390165151)
XLA Ops:
  0.6 69.7 %shard_map.50 = (f32[128,256]{1,0:T(8,128)}, f32[4,4096]{1,0:T(4,128)}) custom-call(bf16[128,256]{1,0:T(8,128)(2,1)} %t_hbm.1, bf16[128,256]{1,0:T(8,128)(2,1)} %s_hbm.1, bf16[256,4096]{1,0:T(8,128)(2,1)} %w_hbm.1), custom_call_target="tpu_custom_call" | custom-call | tf_op jit(solution)/shard_map/pallas_call | solution.py:478
  70.3 1.6 %shard_map.51 = (f32[128,256]{1,0:T(8,128)}, f32[4,4096]{1,0:T(4,128)}) custom-call(f32[128,256]{1,0:T(8,128)} %get-tuple-element.4.features, f32[4,4096]{1,0:T(4,128)} %get-tuple-element.5.protos), custom_call_target="tpu_custom_call" | custom-call | tf_op jit(solution)/shard_map/pallas_call | solution.py:488

commit v5 on v4

--- a/solution.py
+++ b/solution.py
@@ -22,10 +22,11 @@
 SCALE = 32768 / 64.0 / 0.1
 MESH = pl.DeviceIdType.MESH
 
-UP, DN, G0, GY, G2, TZ, T1, T2, RM, GP, AR, TR, ZA = range(13)
+UP, DN, G0, GY, NO, TZ, T1, T2, RM, GP, AR, TR, ZA = range(13)
 XX, YY, ZZ = (13, 16, 19)
-GL, GR, GF = (22, 24, 26)
-GROUPS = 28
+GL, GR, GF, GH = (22, 24, 26, 28)
+GROUPS = 31
+PARTS = ((1, 2), (3, 2), (5, 3))
 XO = (2, 1, 3)
 YO = ZO = (4, 3, 5, 2, 6, 1, 7)
 LOADS = 4
@@ -48,7 +49,7 @@
 def body(
     t_hbm, s_hbm, w_hbm, gf_out, gp_out,
     t_ref, s_ref, w_ref, WU, E, SE, F, ETB, ESB, SBT, GB, GPS, GPR, GAS, GAR, GTS, GTR, GFO, GFA,
-    CS, CR, XS, XR, YS, YR, CF, ZS, ZRV, ZL, TZS, TZR, TS, RB, RBM, ITB, RW, ITW, lsem, ssem, rsem,
+    CS, CR, XS, XR, YS, YR, CF, ZS, ZRV, ZL, TZS, TZR, TS, RB, RBM, ITB, RW, ITW, lsem, ssem, rsem, phase,
 ):
     dp = lax.axis_index("dp")
     z = lax.axis_index("proto")
@@ -188,22 +189,28 @@
         send(F.at[2 + p, pl.ds(0, B)], F.at[4 + p, pl.ds(0, B)], GF + p, dev(1, 0, 0, 0))
         send(F.at[6 + p, pl.ds(B, B)], F.at[4 + p, pl.ds(B, B)], GF + p, dev(3, 0, 0, 0))
 
-    def gather_1():
+    def to_pair():
         send(F.at[0], F.at[1], GY, dev(0, flip, 0, 0))
-        to_sides(0)
-
-    def gather_2():
+
+    def second_row():
         arrived(F.at[1], GY)
         to_sides(1)
         relay(0)
 
-    def gather_3():
-        relay(1)
-
-    def gather_4():
-        for p in range(2):
-            arrived(F.at[4 + p], GF + p)
-        send(F.at[pl.ds(1, NB - 1)], F.at[pl.ds(NB + 1, NB - 1)], G2, mate)
+    def hand(part):
+        lo, count = PARTS[part]
+        send(F.at[pl.ds(lo, count)], F.at[pl.ds(NB + lo, count)], GH + part, mate)
+
+    def handed(part):
+        lo, count = PARTS[part]
+        arrived(F.at[pl.ds(NB + lo, count)], GH + part)
+        blocks(NB + lo, NB + lo + count)
+
+    def idle(point):
+        pl.semaphore_signal(phase.at[point], inc=1, device_id=mate, device_id_type=MESH)
+
+    def when_idle(point):
+        pl.semaphore_wait(phase.at[point], 1)
 
     own = (x * 2 + lax.rem(y, 2)) * NC + c
 
@@ -224,22 +231,34 @@
     def _():
         send(CS, CR, UP, mate)
         send(F.at[0], F.at[NB], G0, mate)
-        gather_1()
         student()
+        when_idle(0)
+        to_sides(0)
+        student_totals()
+        when_idle(1)
+        to_pair()
+        arrived(F.at[NB], G0)
+        blocks(NB, NB + 1)
         blocks(0, 1)
-        student_totals()
-        arrived(F.at[NB], G0)
-        gather_2()
-        blocks(NB, NB + 1)
-        blocks(1, 2)
-        gather_3()
         hand_totals()
+        when_idle(2)
+        second_row()
         student_product()
+        hand(0)
+        blocks(1, 3)
         line_totals()
-        gather_4()
-        blocks(2, NB)
-        arrived(F.at[pl.ds(NB + 1, NB - 1)], G2)
-        blocks(NB + 1, 2 * NB)
+        arrived(F.at[4], GF)
+        blocks(4, 5)
+        when_idle(3)
+        relay(1)
+        hand(1)
+        blocks(3, 4)
+        blocks(6, 8)
+        arrived(F.at[5], GF + 1)
+        hand(2)
+        blocks(5, 6)
+        for part in range(3):
+            handed(part)
         arrived(CF.at[last], DN)
         teacher_product()
         arrived(RB, RM)
@@ -260,27 +279,35 @@
             for k in XO:
                 send(XS.at[i], XR.at[i, k - 1], XX + i, dev(k, 0, 0, 0))
             if i == 0:
-                gather_1()
                 arrived(F.at[NB], G0)
                 lax.fori_loop(0, CH, mate_exp, 0, unroll=4)
             elif i == 1:
-                blocks(0, 2)
+                blocks(0, 1)
                 blocks(NB, NB + 1)
                 hand_totals()
             else:
-                blocks(2, NB)
+                hand(0)
+                blocks(1, 3)
             arrived(XR.at[i], XX + i)
             YS[i] = (XS[i] + XR[i, 0]) + (XR[i, 1] + XR[i, 2])
             for k in YO:
                 send(YS.at[i], YR.at[i, k - 1], YY + i, dev(0, k, 0, 0))
             if i == 0:
+                idle(0)
+                to_sides(0)
                 student()
             elif i == 1:
-                gather_3()
+                idle(2)
+                second_row()
                 student_product()
             else:
-                arrived(F.at[pl.ds(NB + 1, NB - 1)], G2)
-                blocks(NB + 1, 2 * NB)
+                idle(3)
+                relay(1)
+                arrived(F.at[4], GF)
+                hand(1)
+                blocks(3, 5)
+                blocks(6, 8)
+                handed(0)
             arrived(YR.at[i], YY + i)
             total = YS[i]
             for k in range(NY - 1):
@@ -299,10 +326,10 @@
                 for k in ZO:
                     send(ZS.at[i], ZRV.at[i, k - 1], ZZ + i, dev(0, 0, 0, k))
                 if i == 0:
+                    idle(1)
+                    to_pair()
                     student_totals()
-                    gather_2()
                 else:
-                    gather_4()
                     line_totals()
                 arrived(ZRV.at[i], ZZ + i)
                 total = ZS[i]
@@ -325,6 +352,11 @@
                     send(ZS.at[i], ZL.at[k], ZZ + i, to)
                 ZL[0] = ZS[i]
                 teacher_product()
+                arrived(F.at[5], GF + 1)
+                hand(2)
+                blocks(5, 6)
+                handed(1)
+                handed(2)
                 arrived(ZL.at[pl.ds(1, NB * NZ - 1)], ZZ + i)
                 for j in range(NB):
                     total = ZL[j * NZ]
@@ -414,7 +446,8 @@
         sent(F.at[p], GL + p)
         sent(F.at[p], GR + p)
         sent(F.at[4 + p], GF + p)
-    sent(F.at[pl.ds(1, NB - 1)], G2)
+    for part, (lo, count) in enumerate(PARTS):
+        sent(F.at[pl.ds(lo, count)], GH + part)
     sent(TS.at[pl.ds(1, NB - 1)], T1)
     sent(TS.at[pl.ds(0, NB)], T2)
     sent(GPR.at[pl.ds(1, NX * NY * NC - 1)], GP)
@@ -472,6 +505,7 @@
         pltpu.SemaphoreType.DMA((2 + LOADS,)),
         pltpu.SemaphoreType.DMA((GROUPS,)),
         pltpu.SemaphoreType.DMA((GROUPS,)),
+        pltpu.SemaphoreType.REGULAR((4,)),
     ]
     whole = pl.BlockSpec(memory_space=pltpu.VMEM)
     anywhere = pl.BlockSpec(memory_space=pl.ANY)

time: 72.1 us -> 68.9 us (0.956); the launches traced: 71.9 us -> 67.7 us
  Pallas kernels: 71.3 us -> 67.1 us
    pallas_call x1, Pallas kernels: 69.7 us -> 65.5 us  [shards(): pl.pallas_call(body, out_shape=(jax.ShapeDtypeStruct((B, D), f32), jax.Sh...]
where the time goes in v5:
time: 68.9 us; the launch traced here: 67.7 us
  Pallas kernels  67.1 us (97%)
    pallas_call x1, Pallas kernels, shards(): pl.pallas_call(body, out_shape=(jax.ShapeDtypeStruct((B, D), f32), jax.Sh...  65.5 us
    pallas_call x1, Pallas kernels, shards(): pl.pallas_call(place, out_shape=tuple((jax.ShapeDtypeStruct(g.shape, g.dt...  1.59 us

profile of v5, /device:TPU:1, one launch (start us, length us, event | category | flops | bytes accessed | tf_op | source)
XLA Modules:
  0.0 67.7 jit_solution(17574924690691934639)
XLA Ops:
  0.6 65.5 %shard_map.50 = (f32[128,256]{1,0:T(8,128)}, f32[4,4096]{1,0:T(4,128)}) custom-call(bf16[128,256]{1,0:T(8,128)(2,1)} %t_hbm.1, bf16[128,256]{1,0:T(8,128)(2,1)} %s_hbm.1, bf16[256,4096]{1,0:T(8,128)(2,1)} %w_hbm.1), custom_call_target="tpu_custom_call" | custom-call | tf_op jit(solution)/shard_map/pallas_call | solution.py:512
  66.1 1.6 %shard_map.51 = (f32[128,256]{1,0:T(8,128)}, f32[4,4096]{1,0:T(4,128)}) custom-call(f32[128,256]{1,0:T(8,128)} %get-tuple-element.4.features, f32[4,4096]{1,0:T(4,128)} %get-tuple-element.5.protos), custom_call_target="tpu_custom_call" | custom-call | tf_op jit(solution)/shard_map/pallas_call | solution.py:522

commit v6 on v5

--- a/solution.py
+++ b/solution.py
@@ -81,13 +81,11 @@
             ref, ref, ssem.at[group], rsem.at[group], device_id=mate, device_id_type=MESH
         ).wait_send()
 
-    loads = [
-        pltpu.make_async_copy(t_hbm, t_ref, lsem.at[0]),
-        pltpu.make_async_copy(s_hbm, s_ref, lsem.at[1]),
-    ]
+    loads = [pltpu.make_async_copy(t_hbm, t_ref, lsem.at[0])]
     for piece in range(LOADS):
         cols = pl.ds(piece * (K // LOADS), K // LOADS)
-        loads.append(pltpu.make_async_copy(w_hbm.at[:, cols], w_ref.at[:, cols], lsem.at[2 + piece]))
+        loads.append(pltpu.make_async_copy(w_hbm.at[:, cols], w_ref.at[:, cols], lsem.at[1 + piece]))
+    loads.append(pltpu.make_async_copy(s_hbm, s_ref, lsem.at[1 + LOADS]))
     for load in loads:
         load.start()
 
@@ -117,9 +115,9 @@
 
     per = CH // LOADS
     for piece in range(LOADS):
-        loads[2 + piece].wait()
+        loads[1 + piece].wait()
         lax.fori_loop(piece * per, piece * per + per, first, 0, unroll=True)
-    loads[1].wait()
+    loads[1 + LOADS].wait()
     s_unit, _ = unit_rows(s_ref[...])
     F[0, B:, :] = s_unit.astype(jnp.float32)
     pl.semaphore_wait(barrier, len(peers))
@@ -145,7 +143,7 @@
                 jnp.concatenate([high, low], 0), WU[j], (((1,), (1,)), ((), ())), preferred_element_type=jnp.float32
             )
 
-        acc = lax.fori_loop(0, CH, step, jnp.zeros((2 * B, D), jnp.float32), unroll=2)
+        acc = lax.fori_loop(0, CH, step, jnp.zeros((2 * B, D), jnp.float32), unroll=4)
         GFA[...] = acc[:B] + acc[B:]
         for k in range(NZ):
             kept[k] = GFA[16 * k:16 * k + 16, :]
@@ -257,10 +255,11 @@
         arrived(F.at[5], GF + 1)
         hand(2)
         blocks(5, 6)
-        for part in range(3):
-            handed(part)
+        handed(0)
         arrived(CF.at[last], DN)
         teacher_product()
+        handed(1)
+        handed(2)
         arrived(RB, RM)
 
     @pl.when(c == 1)
@@ -319,7 +318,7 @@
             def step(t, acc):
                 return acc + E[t] * CF[i, pl.ds(t, 1), :]
 
-            acc = lax.fori_loop(0, TL, step, jnp.zeros((2 * B, 128), jnp.float32), unroll=4)
+            acc = lax.fori_loop(0, TL, step, jnp.zeros((2 * B, 128), jnp.float32), unroll=8)
             ZS[i, 0:1, :] = jnp.sum(acc[:B].T, 0, keepdims=True)
             ZS[i, 1:2, :] = jnp.sum(acc[B:].T, 0, keepdims=True)
             if i < last:
@@ -344,16 +343,16 @@
                     XS[i + 1, pl.ds(t, 1), :] = jnp.sum(e[:B] + e[B:], 0, keepdims=True)
                     return carry
 
-                lax.fori_loop(0, TL, scaled, 0, unroll=4)
+                lax.fori_loop(0, TL, scaled, 0, unroll=8)
             else:
                 far = lambda k: -(min(k // (2 * NZ), NX - k // (2 * NZ)) + k // NZ % 2 + min(k % NZ, NZ - k % NZ))
                 for k in sorted(range(1, NB * NZ), key=far):
                     to = dev(k // (2 * NZ), flip * (k // NZ % 2), 0, k % NZ)
                     send(ZS.at[i], ZL.at[k], ZZ + i, to)
                 ZL[0] = ZS[i]
-                teacher_product()
                 arrived(F.at[5], GF + 1)
                 hand(2)
+                teacher_product()
                 blocks(5, 6)
                 handed(1)
                 handed(2)
@@ -378,7 +377,7 @@
             GB[j, :, 128 * q:128 * q + 128] = g.astype(jnp.bfloat16)
         return carry
 
-    lax.fori_loop(0, 2 * NB, line_grad, 0, unroll=4)
+    lax.fori_loop(0, 2 * NB, line_grad, 0, unroll=True)
     acc = jnp.zeros((D, KB), jnp.float32)
     for p in range(NB):
         lhs = jnp.concatenate([SBT[2 * p], SBT[2 * p + 1]], 1)

time: 68.9 us -> 67.4 us (0.978); the launches traced: 67.7 us -> 67.3 us
  no operation moved by 1% of the time
where the time goes in v6:
time: 67.4 us; the launch traced here: 67.3 us
  Pallas kernels  66.6 us (99%)
    pallas_call x1, Pallas kernels, shards(): pl.pallas_call(body, out_shape=(jax.ShapeDtypeStruct((B, D), f32), jax.Sh...  65 us
    pallas_call x1, Pallas kernels, shards(): pl.pallas_call(place, out_shape=tuple((jax.ShapeDtypeStruct(g.shape, g.dt...  1.59 us

profile of v6, /device:TPU:1, one launch (start us, length us, event | category | flops | bytes accessed | tf_op | source)
XLA Modules:
  0.0 67.3 jit_solution(8652133911548142788)
XLA Ops:
  0.6 65.0 %shard_map.50 = (f32[128,256]{1,0:T(8,128)}, f32[4,4096]{1,0:T(4,128)}) custom-call(bf16[128,256]{1,0:T(8,128)(2,1)} %t_hbm.1, bf16[128,256]{1,0:T(8,128)(2,1)} %s_hbm.1, bf16[256,4096]{1,0:T(8,128)(2,1)} %w_hbm.1), custom_call_target="tpu_custom_call" | custom-call | tf_op jit(solution)/shard_map/pallas_call | solution.py:511
  65.7 1.6 %shard_map.51 = (f32[128,256]{1,0:T(8,128)}, f32[4,4096]{1,0:T(4,128)}) custom-call(f32[128,256]{1,0:T(8,128)} %get-tuple-element.4.features, f32[4,4096]{1,0:T(4,128)} %get-tuple-element.5.protos), custom_call_target="tpu_custom_call" | custom-call | tf_op jit(solution)/shard_map/pallas_call | solution.py:521

commit v7 on v6

--- a/solution.py
+++ b/solution.py
@@ -81,6 +81,16 @@
             ref, ref, ssem.at[group], rsem.at[group], device_id=mate, device_id_type=MESH
         ).wait_send()
 
+    barrier = pltpu.get_barrier_semaphore()
+    peers = [(0, k, 0, 0) for k in YO] + [(0, 0, 0, k) for k in ZO] + [(k, 0, 0, 0) for k in XO]
+    peers = sorted(peers, key=lambda o: -(min(o[0], NX - o[0]) + min(o[1], NY - o[1]) + min(o[3], NZ - o[3])))
+    pl.semaphore_signal(barrier, inc=1, device_id=mate, device_id_type=MESH)
+
+    @pl.when(c == 1)
+    def _():
+        for offset in peers:
+            pl.semaphore_signal(barrier, inc=1, device_id=dev(*offset), device_id_type=MESH)
+
     loads = [pltpu.make_async_copy(t_hbm, t_ref, lsem.at[0])]
     for piece in range(LOADS):
         cols = pl.ds(piece * (K // LOADS), K // LOADS)
@@ -88,15 +98,6 @@
     loads.append(pltpu.make_async_copy(s_hbm, s_ref, lsem.at[1 + LOADS]))
     for load in loads:
         load.start()
-
-    peers = [dev(0, 0, 1, 0)]
-    peers += [dev(k, 0, 0, 0) for k in range(1, NX)]
-    peers += [dev(0, k, 0, 0) for k in range(1, NY)]
-    peers += [dev(0, 0, 0, k) for k in range(1, NZ)]
-    peers += [dev(k, flip, 0, 0) for k in range(1, NX)]
-    barrier = pltpu.get_barrier_semaphore()
-    for to in peers:
-        pl.semaphore_signal(barrier, inc=1, device_id=to, device_id_type=MESH)
 
     loads[0].wait()
     t_unit, _ = unit_rows(t_ref[...])
@@ -120,7 +121,14 @@
     loads[1 + LOADS].wait()
     s_unit, _ = unit_rows(s_ref[...])
     F[0, B:, :] = s_unit.astype(jnp.float32)
-    pl.semaphore_wait(barrier, len(peers))
+
+    @pl.when(c == 0)
+    def _():
+        pl.semaphore_wait(barrier, 1)
+
+    @pl.when(c == 1)
+    def _():
+        pl.semaphore_wait(barrier, 1 + len(peers))
 
     def student():
         def step(j, acc):
@@ -131,6 +139,8 @@
 
         acc = lax.fori_loop(0, CH, step, jnp.zeros((B, 128), jnp.float32), unroll=4)
         TZS[...] = jnp.sum(acc.T, 0, keepdims=True)
+
+    def exchange_totals():
         for k in ZO:
             send(TZS, TZR.at[k - 1], TZ, dev(0, 0, 0, k))
 
@@ -232,16 +242,18 @@
         student()
         when_idle(0)
         to_sides(0)
-        student_totals()
         when_idle(1)
         to_pair()
         arrived(F.at[NB], G0)
         blocks(NB, NB + 1)
         blocks(0, 1)
-        hand_totals()
+        when_idle(4)
+        exchange_totals()
         when_idle(2)
         second_row()
+        student_totals()
         student_product()
+        hand_totals()
         hand(0)
         blocks(1, 3)
         line_totals()
@@ -286,6 +298,7 @@
                 hand_totals()
             else:
                 hand(0)
+                line_totals()
                 blocks(1, 3)
             arrived(XR.at[i], XX + i)
             YS[i] = (XS[i] + XR[i, 0]) + (XR[i, 1] + XR[i, 2])
@@ -295,6 +308,7 @@
                 idle(0)
                 to_sides(0)
                 student()
+                exchange_totals()
             elif i == 1:
                 idle(2)
                 second_row()
@@ -328,9 +342,9 @@
                     idle(1)
                     to_pair()
                     student_totals()
-                else:
-                    line_totals()
                 arrived(ZRV.at[i], ZZ + i)
+                if i == 0:
+                    idle(4)
                 total = ZS[i]
                 for k in range(NZ - 1):
                     total = total + ZRV[i, k]
@@ -504,7 +518,7 @@
         pltpu.SemaphoreType.DMA((2 + LOADS,)),
         pltpu.SemaphoreType.DMA((GROUPS,)),
         pltpu.SemaphoreType.DMA((GROUPS,)),
-        pltpu.SemaphoreType.REGULAR((4,)),
+        pltpu.SemaphoreType.REGULAR((5,)),
     ]
     whole = pl.BlockSpec(memory_space=pltpu.VMEM)
     anywhere = pl.BlockSpec(memory_space=pl.ANY)

time: 67.4 us -> 68.5 us (1.016)
  Pallas kernels: 66.6 us -> 67.7 us
    pallas_call x1, Pallas kernels: 65 us -> 66.1 us  [shards(): pl.pallas_call(body, out_shape=(jax.ShapeDtypeStruct((B, D), f32), jax.Sh...]
where the time goes in v7:
time: 68.5 us; the launch traced here: 68.3 us
  Pallas kernels  67.7 us (99%)
    pallas_call x1, Pallas kernels, shards(): pl.pallas_call(body, out_shape=(jax.ShapeDtypeStruct((B, D), f32), jax.Sh...  66.1 us
    pallas_call x1, Pallas kernels, shards(): pl.pallas_call(place, out_shape=tuple((jax.ShapeDtypeStruct(g.shape, g.dt...  1.59 us

profile of v7, /device:TPU:1, one launch (start us, length us, event | category | flops | bytes accessed | tf_op | source)
XLA Modules:
  0.0 68.3 jit_solution(18265298863468411437)
XLA Ops:
  0.6 66.1 %shard_map.50 = (f32[128,256]{1,0:T(8,128)}, f32[4,4096]{1,0:T(4,128)}) custom-call(bf16[128,256]{1,0:T(8,128)(2,1)} %t_hbm.1, bf16[128,256]{1,0:T(8,128)(2,1)} %s_hbm.1, bf16[256,4096]{1,0:T(8,128)(2,1)} %w_hbm.1), custom_call_target="tpu_custom_call" | custom-call | tf_op jit(solution)/shard_map/pallas_call | solution.py:525
  66.7 1.6 %shard_map.51 = (f32[128,256]{1,0:T(8,128)}, f32[4,4096]{1,0:T(4,128)}) custom-call(f32[128,256]{1,0:T(8,128)} %get-tuple-element.4.features, f32[4,4096]{1,0:T(4,128)} %get-tuple-element.5.protos), custom_call_target="tpu_custom_call" | custom-call | tf_op jit(solution)/shard_map/pallas_call | solution.py:535

commit v8 on v6

--- a/solution.py
+++ b/solution.py
@@ -81,6 +81,13 @@
             ref, ref, ssem.at[group], rsem.at[group], device_id=mate, device_id_type=MESH
         ).wait_send()
 
+    offsets = [(0, k, 0, 0) for k in YO] + [(0, 0, 0, k) for k in ZO] + [(k, 0, 0, 0) for k in XO]
+    offsets = sorted(offsets, key=lambda o: -(min(o[0], NX - o[0]) + min(o[1], NY - o[1]) + min(o[3], NZ - o[3])))
+    peers = [dev(k, flip, 0, 0) for k in XO] + [dev(*o) for o in offsets] + [mate]
+    barrier = pltpu.get_barrier_semaphore()
+    for to in peers:
+        pl.semaphore_signal(barrier, inc=1, device_id=to, device_id_type=MESH)
+
     loads = [pltpu.make_async_copy(t_hbm, t_ref, lsem.at[0])]
     for piece in range(LOADS):
         cols = pl.ds(piece * (K // LOADS), K // LOADS)
@@ -88,15 +95,6 @@
     loads.append(pltpu.make_async_copy(s_hbm, s_ref, lsem.at[1 + LOADS]))
     for load in loads:
         load.start()
-
-    peers = [dev(0, 0, 1, 0)]
-    peers += [dev(k, 0, 0, 0) for k in range(1, NX)]
-    peers += [dev(0, k, 0, 0) for k in range(1, NY)]
-    peers += [dev(0, 0, 0, k) for k in range(1, NZ)]
-    peers += [dev(k, flip, 0, 0) for k in range(1, NX)]
-    barrier = pltpu.get_barrier_semaphore()
-    for to in peers:
-        pl.semaphore_signal(barrier, inc=1, device_id=to, device_id_type=MESH)
 
     loads[0].wait()
     t_unit, _ = unit_rows(t_ref[...])
@@ -304,9 +302,6 @@
                 relay(1)
                 arrived(F.at[4], GF)
                 hand(1)
-                blocks(3, 5)
-                blocks(6, 8)
-                handed(0)
             arrived(YR.at[i], YY + i)
             total = YS[i]
             for k in range(NY - 1):
@@ -353,7 +348,8 @@
                 arrived(F.at[5], GF + 1)
                 hand(2)
                 teacher_product()
-                blocks(5, 6)
+                blocks(3, NB)
+                handed(0)
                 handed(1)
                 handed(2)
                 arrived(ZL.at[pl.ds(1, NB * NZ - 1)], ZZ + i)

time: 67.4 us -> 67.3 us (level)
  no operation moved by 1% of the time
where the time goes in v8:
time: 67.3 us; the launch traced here: 67.2 us
  Pallas kernels  66.5 us (99%)
    pallas_call x1, Pallas kernels, shards(): pl.pallas_call(body, out_shape=(jax.ShapeDtypeStruct((B, D), f32), jax.Sh...  65 us
    pallas_call x1, Pallas kernels, shards(): pl.pallas_call(place, out_shape=tuple((jax.ShapeDtypeStruct(g.shape, g.dt...  1.59 us

profile of v8, /device:TPU:1, one launch (start us, length us, event | category | flops | bytes accessed | tf_op | source)
XLA Modules:
  0.0 67.2 jit_solution(462775343227510176)
XLA Ops:
  0.6 65.0 %shard_map.50 = (f32[128,256]{1,0:T(8,128)}, f32[4,4096]{1,0:T(4,128)}) custom-call(bf16[128,256]{1,0:T(8,128)(2,1)} %t_hbm.1, bf16[128,256]{1,0:T(8,128)(2,1)} %s_hbm.1, bf16[256,4096]{1,0:T(8,128)(2,1)} %w_hbm.1), custom_call_target="tpu_custom_call" | custom-call | tf_op jit(solution)/shard_map/pallas_call | solution.py:507
  65.6 1.6 %shard_map.51 = (f32[128,256]{1,0:T(8,128)}, f32[4,4096]{1,0:T(4,128)}) custom-call(f32[128,256]{1,0:T(8,128)} %get-tuple-element.4.features, f32[4,4096]{1,0:T(4,128)} %get-tuple-element.5.protos), custom_call_target="tpu_custom_call" | custom-call | tf_op jit(solution)/shard_map/pallas_call | solution.py:517

commit v9 on v8

--- a/solution.py
+++ b/solution.py
@@ -222,6 +222,16 @@
         lax.fori_loop(lo, hi, line_block, 0)
 
     last = ITERS - 1
+
+    def weigh_blocks():
+        def step(j, carry):
+            for q in range(KB // 128):
+                part = pl.ds(128 * q, 128)
+                ESB[j, :, part] = ESB[j, :, part] * ITB[j]
+                ETB[j, :, part] = ETB[j, :, part] * CF[last, pl.ds(own * (KB // 128) + q, 1), :]
+            return carry
+
+        lax.fori_loop(0, 2 * NB, step, 0, unroll=2)
 
     @pl.when(c == 0)
     def _():
@@ -258,6 +268,7 @@
         teacher_product()
         handed(1)
         handed(2)
+        weigh_blocks()
         arrived(RB, RM)
 
     @pl.when(c == 1)
@@ -352,6 +363,7 @@
                 handed(0)
                 handed(1)
                 handed(2)
+                weigh_blocks()
                 arrived(ZL.at[pl.ds(1, NB * NZ - 1)], ZZ + i)
                 for j in range(NB):
                     total = ZL[j * NZ]
@@ -368,8 +380,7 @@
         rb = across(RB[j] * SCALE)
         for q in range(KB // 128):
             part = pl.ds(128 * q, 128)
-            col = CF[last, pl.ds(own * (KB // 128) + q, 1), :]
-            g = ESB[j, :, part] * ITB[j] - (ETB[j, :, part] * col) * rb
+            g = ESB[j, :, part] - ETB[j, :, part] * rb
             GB[j, :, 128 * q:128 * q + 128] = g.astype(jnp.bfloat16)
         return carry
 
@@ -451,9 +462,22 @@
     sent(GFO.at[pl.ds(1, NZ - 1)], ZA)
 
 
-def place(features, protos, features_out, protos_out):
-    features_out[...] = features[...]
-    protos_out[...] = protos[...]
+def place(features, protos, features_out, protos_out, features_held, protos_held, sem):
+    into = [
+        pltpu.make_async_copy(features, features_held, sem.at[0]),
+        pltpu.make_async_copy(protos, protos_held, sem.at[1]),
+    ]
+    out = [
+        pltpu.make_async_copy(features_held, features_out, sem.at[2]),
+        pltpu.make_async_copy(protos_held, protos_out, sem.at[3]),
+    ]
+    for copy in into:
+        copy.start()
+    for k in (1, 0):
+        into[k].wait()
+        out[k].start()
+    for copy in out:
+        copy.wait()
 
 
 def shards(teacher, student, protos):
@@ -517,8 +541,9 @@
     return pl.pallas_call(
         place,
         out_shape=tuple(jax.ShapeDtypeStruct(g.shape, g.dtype) for g in grads),
-        in_specs=[whole] * 2,
-        out_specs=(whole,) * 2,
+        in_specs=[anywhere] * 2,
+        out_specs=(anywhere,) * 2,
+        scratch_shapes=[vm((B, D), f32), vm((4, K), f32), pltpu.SemaphoreType.DMA((4,))],
         compiler_params=pltpu.CompilerParams(vmem_limit_bytes=60 * 2**20),
     )(*grads)
 

time: 67.3 us -> 67.3 us (level)
  no operation moved by 1% of the time
where the time goes in v9:
time: 67.3 us; the launch traced here: 67.1 us
  Pallas kernels  66.5 us (99%)
    pallas_call x1, Pallas kernels, shards(): pl.pallas_call(body, out_shape=(jax.ShapeDtypeStruct((B, D), f32), jax.Sh...  64.9 us
    pallas_call x1, Pallas kernels, shards(): pl.pallas_call(place, out_shape=tuple((jax.ShapeDtypeStruct(g.shape, g.dt...  1.61 us

profile of v9, /device:TPU:1, one launch (start us, length us, event | category | flops | bytes accessed | tf_op | source)
XLA Modules:
  0.0 67.1 jit_solution(15903341838734795362)
XLA Ops:
  0.6 64.9 %shard_map.50 = (f32[128,256]{1,0:T(8,128)}, f32[4,4096]{1,0:T(4,128)}) custom-call(bf16[128,256]{1,0:T(8,128)(2,1)} %t_hbm.1, bf16[128,256]{1,0:T(8,128)(2,1)} %s_hbm.1, bf16[256,4096]{1,0:T(8,128)(2,1)} %w_hbm.1), custom_call_target="tpu_custom_call" | custom-call | tf_op jit(solution)/shard_map/pallas_call | solution.py:531
  65.5 1.6 %shard_map.51 = (f32[128,256]{1,0:T(8,128)}, f32[4,4096]{1,0:T(4,128)}) custom-call(f32[128,256]{1,0:T(8,128)} %get-tuple-element.4.features, f32[4,4096]{1,0:T(4,128)} %get-tuple-element.5.protos), custom_call_target="tpu_custom_call" | custom-call | tf_op jit(solution)/shard_map/pallas_call | solution.py:541

commit v10 on v8

--- a/solution.py
+++ b/solution.py
@@ -29,7 +29,7 @@
 PARTS = ((1, 2), (3, 2), (5, 3))
 XO = (2, 1, 3)
 YO = ZO = (4, 3, 5, 2, 6, 1, 7)
-LOADS = 4
+LOADS = 2
 
 
 def dot(a, b):

time: 67.3 us -> 67.3 us (level)
  no operation moved by 1% of the time
where the time goes in v10:
time: 67.3 us; the launch traced here: 67.2 us
  Pallas kernels  66.5 us (99%)
    pallas_call x1, Pallas kernels, shards(): pl.pallas_call(body, out_shape=(jax.ShapeDtypeStruct((B, D), f32), jax.Sh...  64.9 us
    pallas_call x1, Pallas kernels, shards(): pl.pallas_call(place, out_shape=tuple((jax.ShapeDtypeStruct(g.shape, g.dt...  1.59 us

profile of v10, /device:TPU:1, one launch (start us, length us, event | category | flops | bytes accessed | tf_op | source)
XLA Modules:
  0.0 67.2 jit_solution(13916314175484908164)
XLA Ops:
  0.6 64.9 %shard_map.50 = (f32[128,256]{1,0:T(8,128)}, f32[4,4096]{1,0:T(4,128)}) custom-call(bf16[128,256]{1,0:T(8,128)(2,1)} %t_hbm.1, bf16[128,256]{1,0:T(8,128)(2,1)} %s_hbm.1, bf16[256,4096]{1,0:T(8,128)(2,1)} %w_hbm.1), custom_call_target="tpu_custom_call" | custom-call | tf_op jit(solution)/shard_map/pallas_call | solution.py:507
  65.6 1.6 %shard_map.51 = (f32[128,256]{1,0:T(8,128)}, f32[4,4096]{1,0:T(4,128)}) custom-call(f32[128,256]{1,0:T(8,128)} %get-tuple-element.4.features, f32[4,4096]{1,0:T(4,128)} %get-tuple-element.5.protos), custom_call_target="tpu_custom_call" | custom-call | tf_op jit(solution)/shard_map/pallas_call | solution.py:517
